TPU v7x, 128 devices: a whole 4x4x4 slice. The times are simulated.
128 devices in a mesh: dp: 8 (over y, x_hi), row: 4 (over z), col: 4 (over x_lo, core).
Axes of the slice: x: 4 (x_hi: 2, x_lo: 2; x = x_hi * 2 + x_lo), y: 4, z: 4, core: 2. Of those that a mesh axis runs over, the one named last changes fastest.
Arguments:
- hidden: bfloat16 [8192, 6656], P(('dp', 'row'), 'col'), may hold values from -6 to 6
- weight: bfloat16 [6656, 8192], P('row', 'col'), may hold values from -0.078125 to 0.078125
- upstream: bfloat16 [8192, 8192], P(('dp', 'row'), 'col'), may hold values from -6 to 6
Outputs:
- output: bfloat16 [8192, 8192], P(('dp', 'row'), 'col')
- hidden_grad: bfloat16 [8192, 6656], P(('dp', 'row'), 'col')
- weight_grad: float32 [6656, 8192], P(('row', 'dp'), 'col')
All inputs are finite; a program needn't handle non-finite values.
Results may differ from a plain program's by a relative error of at most 0.015.
Values may be sent and summed in bfloat16 or wider, within the bound.
No kernel may reach another device: no remote copies, remote signals or barrier semaphores. Data moves between devices by JAX's collectives and lax.ppermute only.
A program may use at most 192 MiB of HBM per device.

v0:
```python
import math

import jax
import jax.numpy as jnp
from jax import lax
from jax.sharding import PartitionSpec as P


def shards(hidden, weight, upstream):
    hidden_rows = lax.all_gather(hidden, "col", axis=1, tiled=True)
    block_width = weight.shape[0]
    hidden_all, upstream_all = (
        lax.all_gather(hidden_rows, "row", axis=0, tiled=True),
        lax.all_gather(upstream, "row", axis=0, tiled=True),
    )
    row_index = lax.axis_index("row")
    hidden_block = lax.dynamic_slice_in_dim(hidden_all, row_index * block_width, block_width, 1)
    token_count = lax.axis_size("dp") * lax.axis_size("row") * hidden.shape[0]
    factor = 1.0 / math.sqrt(token_count)
    piece = lax.all_gather(weight, "row", axis=0, tiled=True)
    out_total = jnp.dot(hidden_rows, piece, preferred_element_type=jnp.float32)
    part = lax.dot_general(
        upstream, piece, (((1,), (1,)), ((), ())), preferred_element_type=jnp.float32
    )
    grad_total = part
    out_total, grad_total = (out_total, grad_total)
    output = out_total.astype(jnp.bfloat16)
    hidden_grad = lax.psum_scatter(
        grad_total.astype(jnp.bfloat16), "col", scatter_dimension=1, tiled=True
    )
    weight_part = (
        lax.dot_general(
            hidden_block, upstream_all, (((0,), (0,)), ((), ())), preferred_element_type=jnp.float32
        )
        * factor
    )
    weight_part = weight_part.astype(jnp.bfloat16).astype(jnp.float32)
    weight_grad = lax.psum_scatter(
        weight_part.astype(jnp.bfloat16), "dp", scatter_dimension=0, tiled=True
    ).astype(jnp.float32)
    return (output, hidden_grad, weight_grad)


def solution(mesh):
    return jax.shard_map(
        shards,
        mesh=mesh,
        in_specs=(P(("dp", "row"), "col"), P("row", "col"), P(("dp", "row"), "col")),
        out_specs=(P(("dp", "row"), "col"), P(("dp", "row"), "col"), P(("row", "dp"), "col")),
        check_vma=False,
    )
```

profile of v0, /device:TPU:2, one launch (start us, length us, event | category | flops | bytes accessed | tf_op | source)
XLA Modules:
  0.0 630.9 jit_solution(2992708820219916818)
XLA Ops:
  7.2 0.0 all-gather.5.cloned.1.call-start
  7.2 0.7 all-gather.5.cloned.1.call-update
  7.9 0.0 all-gather.11.cloned.1.call-start
  7.9 0.7 all-gather.11.cloned.1.call-update
  8.6 0.0 all-gather.9.cloned.1.call-start
  8.7 41.7 %all-gather.5.cloned.1.call-done = bf16[256,6656]{1,0:T(8,128)(2,1)} async-done(((bf16[256,1664]{1,0:T(8,128)(2,1)}), bf16[256,6656]{1,0:T(8,128)(2,1)}) %all-gather.5.cloned.1.call-update) | async-done | bytes 3407888 | tf_op jit(solution)/shard_map/all_gather | solution.py:10
  50.4 0.0 all-gather.9.cloned.1.call-update
  50.4 0.0 all-gather.7.cloned.1.call-start
  50.4 0.5 all-gather.7.cloned.1.call-update
  51.0 0.0 reduce-scatter.5.cloned.1.call-start
  51.0 52.1 %all-gather.11.cloned.1.call-done = bf16[1024,2048]{1,0:T(8,128)(2,1)} async-done(((bf16[256,2048]{1,0:T(8,128)(2,1)}), bf16[1024,2048]{1,0:T(8,128)(2,1)}) %all-gather.11.cloned.1.call-update) | async-done | bytes 4194320 | tf_op jit(solution)/shard_map/all_gather | solution.py:14
  103.1 129.4 %all-gather.9.cloned.1.call-done = bf16[1024,6656]{1,0:T(8,128)(2,1)} async-done(((bf16[256,6656]{1,0:T(8,128)(2,1)}), bf16[1024,6656]{1,0:T(8,128)(2,1)}) %all-gather.9.cloned.1.call-update) | async-done | bytes 13631504 | tf_op jit(solution)/shard_map/all_gather | solution.py:13
  232.5 12.0 %multiply_convert_fusion = bf16[1664,2048]{1,0:T(8,128)(2,1)} fusion(bf16[1024,2048]{1,0:T(8,128)(2,1)} %all-gather.11.cloned.1.call-done, bf16[1024,6656]{1,0:T(8,128)(2,1)} %all-gather.9.cloned.1.call-done, s32[]{:T(128)S(6)} %select_n.3), kind=kOutput, calls=%fused_computation | convolution fusion | flops 6986137600 | bytes 14417924 | tf_op jit(solution)/shard_map/dot_general | solution.py:32
  244.5 0.0 copy-start.1
  244.5 0.0 reduce-scatter.5.cloned.1.call-update
  244.5 0.0 reduce-scatter.7.cloned.1.call-start
  244.6 231.7 %all-gather.7.cloned.1.call-done = bf16[6656,2048]{1,0:T(8,128)(2,1)} async-done(((bf16[1664,2048]{1,0:T(8,128)(2,1)}), bf16[6656,2048]{1,0:T(8,128)(2,1)}) %all-gather.7.cloned.1.call-update) | async-done | bytes 27262992 | tf_op jit(solution)/shard_map/all_gather | solution.py:20
  476.2 0.0 copy-done.1
  476.2 13.7 %convolution_convert_fusion = bf16[256,6656]{1,0:T(8,128)(2,1)} fusion(bf16[256,2048]{1,0:T(8,128)(2,1)S(1)} %copy-done.1, bf16[6656,2048]{1,0:T(8,128)(2,1)} %all-gather.7.cloned.1.call-done), kind=kOutput, calls=%fused_computation.1 | convolution fusion | flops 6981025792 | bytes 31719424 | tf_op jit(solution)/shard_map/dot_general | solution.py:22
  490.0 0.0 copy-start
  490.0 6.2 copy.6
  496.1 0.0 reduce-scatter.7.cloned.1.call-update
  496.2 86.7 %reduce-scatter.5.cloned.1.call-done = bf16[208,2048]{1,0:T(8,128)(2,1)} async-done(((bf16[1664,2048]{1,0:T(8,128)(2,1)}), bf16[208,2048]{1,0:T(8,128)(2,1)}) %reduce-scatter.5.cloned.1.call-update) | async-done | bytes 851984 | tf_op jit(solution)/shard_map/reduce_scatter | solution.py:38
  582.9 2.5 convert_element_type.17
  585.4 0.0 copy-done
  585.4 14.5 %convolution_convert_fusion.1 = bf16[256,2048]{1,0:T(8,128)(2,1)} fusion(bf16[256,6656]{1,0:T(8,128)(2,1)S(1)} %copy-done, bf16[6656,2048]{1,0:T(8,128)(2,1)} %all-gather.7.cloned.1.call-done), kind=kOutput, calls=%fused_computation.3 | convolution fusion | flops 6979846144 | bytes 31719424 | tf_op jit(solution)/shard_map/dot_general | solution.py:21
  599.9 22.0 %reduce-scatter.7.cloned.1.call-done = bf16[1664,256]{1,0:T(8,128)(2,1)} async-done(((bf16[6656,256]{1,0:T(8,128)(2,1)}), bf16[1664,256]{1,0:T(8,128)(2,1)}) %reduce-scatter.7.cloned.1.call-update) | async-done | bytes 851984
  621.9 2.2 copy.7
Async XLA Ops:
  7.2 43.2 %all-gather.5.cloned.1.call-start = ((), (), s32[]{:S(2)}) async-start(), calls=%async_computation.2 | async-start | bytes 4259840 | tf_op jit(solution)/shard_map/all_gather | solution.py:10
  7.9 95.2 %all-gather.11.cloned.1.call-start = ((), (), s32[]{:S(2)}) async-start(), calls=%async_computation.5 | async-start | bytes 5242880 | tf_op jit(solution)/shard_map/all_gather | solution.py:14
  8.6 223.9 %all-gather.9.cloned.1.call-start = ((), (), s32[]{:S(2)}) async-start(), calls=%async_computation.4 | async-start | bytes 17039360 | tf_op jit(solution)/shard_map/all_gather | solution.py:13
  50.4 425.9 %all-gather.7.cloned.1.call-start = ((), (), s32[]{:S(2)}) async-start(), calls=%async_computation.3 | async-start | bytes 34078720 | tf_op jit(solution)/shard_map/all_gather | solution.py:20
  51.0 531.9 %reduce-scatter.5.cloned.1.call-start = ((), (), s32[]{:S(2)}) async-start(), calls=%async_computation.6 | async-start | bytes 7667712 | tf_op jit(solution)/shard_map/reduce_scatter | solution.py:38
  244.5 231.7 %copy-start.1 = (bf16[256,2048]{1,0:T(8,128)(2,1)S(1)}, bf16[256,2048]{1,0:T(8,128)(2,1)}, u32[]{:S(2)}) copy-start(bf16[256,2048]{1,0:T(8,128)(2,1)} %param.5) | copy-start | bytes 3145732
  244.5 377.4 %reduce-scatter.7.cloned.1.call-start = ((), (), s32[]{:S(2)}) async-start(), calls=%async_computation.7 | async-start | bytes 4259840
  490.0 95.4 %copy-start = (bf16[256,6656]{1,0:T(8,128)(2,1)S(1)}, bf16[256,6656]{1,0:T(8,128)(2,1)}, u32[]{:S(2)}) copy-start(bf16[256,6656]{1,0:T(8,128)(2,1)} %all-gather.5.cloned.1.call-done) | copy-start | bytes 10223620
Sparse Core Ops, SparseCore 0:
  9.7 40.6 all-gather.4
  52.0 51.0 all-gather.10
  104.8 127.7 all-gather.8
  234.1 242.1 all-gather.6
  480.0 102.8 reduce-scatter.4
  585.1 36.7 reduce-scatter.6
where the time goes:
time: 634 us; the launch traced here: 631 us
  waiting for transfers between devices  566 us (89%)
  matrix products  40.1 us (6%)
  between operations  14.1 us (2%)
  local copies, waits for them, and re-layouts  8.38 us (1%)
    all_gather x1, waiting for transfers between devices, shards(): piece = lax.all_gather(weight, 'row', axis=0, tiled=True)  232 us
    all_gather x1, waiting for transfers between devices, shards(): lax.all_gather(hidden_rows, 'row', axis=0, tiled=True)  129 us
    reduce_scatter x1, waiting for transfers between devices, shards(): lax.psum_scatter(weight_part.astype(jnp.bfloat16), 'dp', scatter_dimensio...  86.7 us
    all_gather x1, waiting for transfers between devices, shards(): lax.all_gather(upstream, 'row', axis=0, tiled=True)  52.1 us
    all_gather x1, waiting for transfers between devices, shards(): hidden_rows = lax.all_gather(hidden, 'col', axis=1, tiled=True)  41.7 us
    unnamed x7, waiting for transfers between devices  24 us
    dot_general x1, matrix products, shards(): out_total = jnp.dot(hidden_rows, piece, preferred_element_type=jnp.float32)  14.5 us
    dot_general x1, matrix products, shards(): lax.dot_general(upstream, piece, (((1,), (1,)), ((), ())), preferred_elem...  13.7 us
  transfers between devices with their start and end apart: 6, of which 6 were waited for; matrix products, arithmetic and copies ran while one was open for 8% of the time, Pallas kernels for 0%

commit v1 on v0

v1 whole, which is shorter than its diff:
```python
import math

import jax
import jax.numpy as jnp
from jax import lax
from jax.sharding import PartitionSpec as P

BF = jnp.bfloat16
F32 = jnp.float32
Z_UP = [(i, (i + 1) % 4) for i in range(4)]
Z_DOWN = [(i, (i + 3) % 4) for i in range(4)]
Y_UP = [(i, (i + 2) % 8) for i in range(8)]
Y_DOWN = [(i, (i + 6) % 8) for i in range(8)]
XHI = [(i, i ^ 1) for i in range(8)]
XLO = [(i, i ^ 2) for i in range(4)]
CORE = [(i, i ^ 1) for i in range(4)]
TO_PLANE = [(t * 4 + f, f * 4 + (t - f) % 4) for t in range(4) for f in range(4)]
FROM_PLANE = [(b, a) for a, b in TO_PLANE]


def dot(a, b, ca, cb):
    return lax.dot_general(a, b, (((ca,), (cb,)), ((), ())), preferred_element_type=F32)


def at(a, i):
    return lax.dynamic_index_in_dim(a, i, 0, keepdims=False)


def pair(first, own, other):
    both = jnp.zeros((2,) + own.shape, own.dtype)
    both = lax.dynamic_update_index_in_dim(both, own, first, 0)
    return lax.dynamic_update_index_in_dim(both, other, 1 - first, 0)


def shards(hidden, weight, upstream):
    d, c = lax.axis_index("dp"), lax.axis_index("col")
    y, xhi, xlo, core = d // 2, d % 2, c // 2, c % 2
    rows, f = hidden.shape
    w = upstream.shape[1]
    half = rows // 2

    h_own = lax.ppermute(hidden, ("row", "col"), TO_PLANE)
    h_x = lax.ppermute(h_own, "col", XLO)
    h_two = pair(xlo, h_own, h_x)
    h_c = lax.ppermute(h_two, "col", CORE)
    h = pair(core, h_two, h_c)
    h = jnp.swapaxes(h, 0, 1).reshape(4 * rows, f)

    u3 = lax.ppermute(upstream, "row", Z_UP)
    u1 = lax.ppermute(upstream, "row", Z_DOWN)
    u2a = lax.ppermute(u3[:half], "row", Z_UP)
    u2b = lax.ppermute(u1[half:], "row", Z_DOWN)
    u = jnp.concatenate([upstream, u1, u2a, u2b, u3], axis=0)

    token_count = lax.axis_size("dp") * lax.axis_size("row") * rows
    factor = 1.0 / math.sqrt(token_count)
    wg = (dot(h, u, 0, 0) * factor).astype(BF).reshape(4, f // 4, w)
    hf = f // 8
    w2 = at(wg, (y + 2) % 4)
    w1 = at(wg, (y + 1) % 4)
    w3 = at(wg, (y + 3) % 4)
    wa = lax.ppermute(w2[:hf], "dp", Y_UP)
    wb = lax.ppermute(w2[hf:], "dp", Y_DOWN)
    s1b = lax.ppermute(w1[hf:], "dp", Y_UP)
    s3a = lax.ppermute(w3[:hf], "dp", Y_DOWN)
    s1a = lax.ppermute((w1[:hf].astype(F32) + wa.astype(F32)).astype(BF), "dp", Y_UP)
    s3b = lax.ppermute((w3[hf:].astype(F32) + wb.astype(F32)).astype(BF), "dp", Y_DOWN)
    w0 = at(wg, y).astype(F32)
    t_a = w0[:hf] + s1a.astype(F32) + s3a.astype(F32)
    t_b = w0[hf:] + s1b.astype(F32) + s3b.astype(F32)
    low = xhi == 0
    x_in = lax.ppermute(jnp.where(low, t_b, t_a).astype(BF), "dp", XHI)
    weight_grad = jnp.where(low, t_a, t_b) + x_in.astype(F32)

    hk = [h[k * rows : (k + 1) * rows] for k in range(4)]
    o2 = dot(hk[2], weight, 1, 0).astype(BF)
    oa = lax.ppermute(o2[:half], "row", Z_UP)
    ob = lax.ppermute(o2[half:], "row", Z_DOWN)
    o1 = dot(hk[1], weight, 1, 0)
    o3 = dot(hk[3], weight, 1, 0)
    o1 = jnp.concatenate([o1[:half] + oa.astype(F32), o1[half:]], axis=0).astype(BF)
    o3 = jnp.concatenate([o3[:half], o3[half:] + ob.astype(F32)], axis=0).astype(BF)
    from_below = lax.ppermute(o1, "row", Z_UP)
    from_above = lax.ppermute(o3, "row", Z_DOWN)
    output = (
        dot(hk[0], weight, 1, 0) + from_below.astype(F32) + from_above.astype(F32)
    ).astype(BF)

    ux = jnp.swapaxes(u.reshape(2, 2, rows, w), 0, 1)
    g_send = dot(at(ux, 1 - core).reshape(2 * rows, w), weight, 1, 1).astype(BF)
    g_in = lax.ppermute(g_send, "col", CORE)
    g = dot(at(ux, core).reshape(2 * rows, w), weight, 1, 1) + g_in.astype(F32)
    g = g.reshape(2, rows, f)
    g_x = lax.ppermute(at(g, 1 - xlo).astype(BF), "col", XLO)
    g = (at(g, xlo) + g_x.astype(F32)).astype(BF)
    hidden_grad = lax.ppermute(g, ("row", "col"), FROM_PLANE)
    return (output, hidden_grad, weight_grad)


def solution(mesh):
    return jax.shard_map(
        shards,
        mesh=mesh,
        in_specs=(P(("dp", "row"), "col"), P("row", "col"), P(("dp", "row"), "col")),
        out_specs=(P(("dp", "row"), "col"), P(("dp", "row"), "col"), P(("row", "dp"), "col")),
        check_vma=False,
    )
```

time: 634 us -> 203 us (0.32)
  waiting for transfers between devices: 566 us -> 115 us
  starting transfers between devices: 0.23 us -> 36.1 us
  between operations: 14.1 us -> 0.96 us
  matrix products: 40.1 us -> 29.7 us
  local copies, waits for them, and re-layouts: 8.38 us -> 15.7 us
    all_gather x4 -> x0, waiting for transfers between devices: 455 us -> none  [the longest x1 232 us: shards(): piece = lax.all_gather(weight, 'row', axis=0, tiled=True)]
    ppermute x0 -> x21, waiting for transfers between devices: none -> 115 us  [the longest x1 37.9 us: shards(): u3 = lax.ppermute(upstream, 'row', Z_UP)]
    reduce_scatter x1 -> x0, waiting for transfers between devices: 86.7 us -> none  [shards(): lax.psum_scatter(weight_part.astype(jnp.bfloat16), 'dp', scatter_dimensio...]
    ppermute x0 -> x21, starting transfers between devices: none -> 36.1 us  [the longest x1 5.23 us: shards(): hidden_grad = lax.ppermute(g, ('row', 'col'), FROM_PLANE)]
    unnamed x7 -> x0, waiting for transfers between devices: 24 us -> none
    dot_general x3 -> x7, matrix products: 40.1 us -> 29.7 us  [dot(): lax.dot_general(a, b, (((ca,), (cb,)), ((), ())), preferred_element_type=...]
  transfers between devices with their start and end apart: 6 -> 21, of which waited for: 6 -> 11; matrix products, arithmetic and copies ran while one was open for 8% -> 23% of each run, Pallas kernels for 0% -> 0%
where the time goes in v1:
time: 203 us; the launch traced here: 202 us
  waiting for transfers between devices  115 us (57%)
  starting transfers between devices  36.1 us (18%)
  matrix products  29.7 us (15%)
  local copies, waits for them, and re-layouts  15.7 us (8%)
  other arithmetic  4.59 us (2%)
    ppermute x1, waiting for transfers between devices, shards(): u3 = lax.ppermute(upstream, 'row', Z_UP)  37.9 us
    dot_general x7, matrix products, dot(): lax.dot_general(a, b, (((ca,), (cb,)), ((), ())), preferred_element_type=...  29.7 us
    ppermute x1, waiting for transfers between devices, shards(): wb = lax.ppermute(w2[hf:], 'dp', Y_DOWN)  23.4 us
    ppermute x1, waiting for transfers between devices, shards(): hidden_grad = lax.ppermute(g, ('row', 'col'), FROM_PLANE)  19 us
    ppermute x1, waiting for transfers between devices, shards(): lax.ppermute((w1[:hf].astype(F32) + wa.astype(F32)).astype(BF), 'dp', Y_UP)  10.9 us
    ppermute x1, waiting for transfers between devices, shards(): u2a = lax.ppermute(u3[:half], 'row', Z_UP)  8.34 us
    unnamed x25, local copies, waits for them, and re-layouts  7.49 us
    ppermute x1, starting transfers between devices, shards(): hidden_grad = lax.ppermute(g, ('row', 'col'), FROM_PLANE)  5.23 us
  transfers between devices with their start and end apart: 21, of which 11 were waited for; matrix products, arithmetic and copies ran while one was open for 23% of the time, Pallas kernels for 0%

profile of v1, /device:TPU:2, one launch (start us, length us, event | category | flops | bytes accessed | tf_op | source)
XLA Modules:
  0.0 202.1 jit_solution(6182716291952524058)
XLA Ops:
  0.6 2.0 collective-permute-start.8
  2.6 2.2 %collective-permute-start.7 = (bf16[256,2048]{1,0:T(8,128)(2,1)}, bf16[256,2048]{1,0:T(8,128)(2,1)S(1)}, u32[]{:S(2)}, u32[]{:S(2)}) collective-permute-start(bf16[256,2048]{1,0:T(8,128)(2,1)} %param.5), channel_id=1, source_target_pairs={{0,12},{4,0},{8,4},{12,8},{1,13},{5,1},{9,5},{13,9},{2,14},{6,2},{... | collective-permute-start | bytes 3145736 | tf_op jit(solution)/shard_map/ppermute | solution.py:50
  4.8 3.7 %collective-permute-start = (bf16[256,1664]{1,0:T(8,128)(2,1)}, bf16[256,1664]{1,0:T(8,128)(2,1)S(1)}, u32[]{:S(2)}, u32[]{:S(2)}) collective-permute-start(bf16[256,1664]{1,0:T(8,128)(2,1)} %param.3), channel_id=1, source_target_pairs={{0,0},{1,7},{2,10},{3,13},{4,1},{5,4},{6,11},{7,14},{8,2},{9,5},{1... | collective-permute-start | bytes 2555912 | tf_op jit(solution)/shard_map/ppermute | solution.py:42
  8.5 37.9 %collective-permute-done.8 = bf16[256,2048]{1,0:T(8,128)(2,1)S(1)} collective-permute-done((bf16[256,2048]{1,0:T(8,128)(2,1)}, bf16[256,2048]{1,0:T(8,128)(2,1)S(1)}, u32[]{:S(2)}, u32[]{:S(2)}) %collective-permute-start.8) | collective-permute-done | bytes 1048608 | tf_op jit(solution)/shard_map/ppermute | solution.py:49
  46.4 0.8 slice.118
  47.2 0.8 slice.119
  48.0 3.2 %collective-permute-start.10 = (bf16[128,2048]{1,0:T(8,128)(2,1)}, bf16[128,2048]{1,0:T(8,128)(2,1)}, u32[]{:S(2)}, u32[]{:S(2)}) collective-permute-start(bf16[128,2048]{1,0:T(8,128)(2,1)} %slice.119), channel_id=1, source_target_pairs={{0,12},{4,0},{8,4},{12,8},{1,13},{5,1},{9,5},{13,9},{2,14},{6,2},{... | collective-permute-start | bytes 1572872 | tf_op jit(solution)/shard_map/ppermute | solution.py:52
  51.3 1.1 constant_dynamic-update-slice_fusion.4
  52.3 1.0 constant_dynamic-update-slice_fusion.3
  53.4 8.3 %collective-permute-done.9 = bf16[128,2048]{1,0:T(8,128)(2,1)S(1)} collective-permute-done((bf16[128,2048]{1,0:T(8,128)(2,1)}, bf16[128,2048]{1,0:T(8,128)(2,1)S(1)}, u32[]{:S(2)}, u32[]{:S(2)}) %collective-permute-start.9) | collective-permute-done | bytes 524320 | tf_op jit(solution)/shard_map/ppermute | solution.py:51
  61.7 0.8 constant_dynamic-update-slice_fusion.2
  62.6 2.5 %constant_dynamic-update-slice_fusion.1 = bf16[1024,2048]{1,0:T(8,128)(2,1)} fusion(bf16[1024,2048]{1,0:T(8,128)(2,1)} %constant_dynamic-update-slice_fusion.2, bf16[128,2048]{1,0:T(8,128)(2,1)} %collective-permute-done.10), kind=kLoop, calls=%fused_computation.49 | loop fusion | bytes 1048576
  65.1 1.1 constant_dynamic-update-slice_fusion
  66.1 2.7 %constant_dynamic-slice_fusion.1 = (bf16[2,1,256,2048]{3,2,1,0:T(8,128)(2,1)S(1)}, bf16[2,1,256,2048]{3,2,1,0:T(8,128)(2,1)S(1)}) fusion(bf16[2,2,256,2048]{3,2,1,0:T(8,128)(2,1)} %bitcast.75, s32[]{:T(128)S(6)} %select_n.79, s32[]{:T(128)S(6)} %select_n.80), kind=kLoop, calls=%fused_computation.54 | loop fusion | bytes 8388616 | tf_op jit(solution)/shard_map/dynamic-slice
  68.8 0.3 slice-done.1
  69.1 5.1 %convolution_convert_fusion = bf16[512,1664]{1,0:T(8,128)(2,1)} fusion(bf16[512,2048]{1,0:T(8,128)(2,1)S(1)} %bitcast.82, bf16[1664,2048]{1,0:T(8,128)(2,1)S(1)} %bitcast.86), kind=kOutput, calls=%fused_computation.2 | convolution fusion | flops 3490512896 | bytes 10616832 | tf_op jit(solution)/shard_map/dot_general | solution.py:22
  74.3 0.1 broadcast_in_dim.21
  74.4 0.1 bitcast_dynamic-update-slice_fusion.3
  74.5 1.3 bitcast_dynamic-update-slice_fusion.2
  75.8 0.6 collective-permute-start.2
  76.4 0.2 broadcast_in_dim.20
  76.7 0.2 bitcast_dynamic-update-slice_fusion
  76.9 1.3 collective-permute-done.11
  78.2 7.5 %convert_add_fusion = f32[512,1664]{1,0:T(8,128)S(1)} fusion(bf16[512,1664]{1,0:T(8,128)(2,1)} %collective-permute-done.11, bf16[512,2048]{1,0:T(8,128)(2,1)S(1)} %bitcast.81, bf16[1664,2048]{1,0:T(8,128)(2,1)} %param.4), kind=kOutput, calls=%fused_computation.1 | convolution fusion | flops 3491364864 | bytes 14024704 | tf_op jit(solution)/shard_map/dot_general | solution.py:22
  85.8 0.1 fusion.11
  85.9 0.3 collective-permute-start.12
  86.2 0.2 bitcast_dynamic-update-slice_fusion.1
  86.5 2.1 %fusion.12 = f32[256,2048]{1,0:T(8,128)S(1)} fusion(bf16[1664,2048]{1,0:T(8,128)(2,1)S(1)} %bitcast.88, bf16[1024,1664]{1,0:T(8,128)(2,1)S(1)} %bitcast.76), kind=kOutput, calls=%fused_computation.40 | convolution fusion | flops 1744830464 | bytes 9764864 | tf_op jit(solution)/shard_map/dot_general | solution.py:22
  88.5 0.7 slice-done.5
  89.2 2.1 %convolution_convert_fusion.1 = bf16[256,2048]{1,0:T(8,128)(2,1)S(1)} fusion(bf16[1664,2048]{1,0:T(8,128)(2,1)S(1)} %bitcast.90, bf16[1024,1664]{1,0:T(8,128)(2,1)S(1)} %bitcast.77), kind=kOutput, calls=%fused_computation.6 | convolution fusion | flops 1745354752 | bytes 8716288 | tf_op jit(solution)/shard_map/dot_general | solution.py:22
  91.3 0.1 copy-done
  91.4 7.7 %multiply_convert_fusion = bf16[1664,2048]{1,0:T(8,128)(2,1)S(1)} fusion(bf16[1024,1664]{1,0:T(8,128)(2,1)S(1)} %bitcast.78, bf16[1024,2048]{1,0:T(8,128)(2,1)S(1)} %copy-done), kind=kOutput, calls=%fused_computation | convolution fusion | flops 6986137600 | bytes 14417920 | tf_op jit(solution)/shard_map/dot_general | solution.py:22
  99.1 0.1 fusion.18
  99.2 2.5 %collective-permute-start.5 = (bf16[128,2048]{1,0:T(8,128)(2,1)S(1)}, bf16[128,2048]{1,0:T(8,128)(2,1)S(1)}, u32[]{:S(2)}, u32[]{:S(2)}) collective-permute-start(bf16[128,2048]{1,0:T(8,128)(2,1)S(1)} %get-tuple-element.12), channel_id=1, source_target_pairs={{0,12},{4,0},{8,4},{12,8},{1,13},{5,1},{9,5},{13,9},{2,14},{6,2},{... | collective-permute-start | bytes 1572872 | tf_op jit(solution)/shard_map/ppermute | solution.py:78
  101.7 2.1 %fusion.15 = f32[256,2048]{1,0:T(8,128)S(1)} fusion(bf16[1664,2048]{1,0:T(8,128)(2,1)S(1)} %bitcast.92, bf16[1024,1664]{1,0:T(8,128)(2,1)S(1)} %bitcast.79), kind=kOutput, calls=%fused_computation.43 | convolution fusion | flops 1744830464 | bytes 9764864 | tf_op jit(solution)/shard_map/dot_general | solution.py:22
  103.8 0.1 collective-permute-start.3
  103.9 0.3 dynamic-slice_bitcast_fusion.2
  104.3 3.1 %collective-permute-start.16 = (bf16[208,2048]{1,0:T(8,128)(2,1)S(1)}, bf16[208,2048]{1,0:T(8,128)(2,1)S(1)}, u32[]{:S(2)}, u32[]{:S(2)}) collective-permute-start(bf16[208,2048]{1,0:T(8,128)(2,1)S(1)} %get-tuple-element.4), channel_id=1, source_target_pairs={{0,96},{16,112},{32,0},{48,16},{64,32},{80,48},{96,64},{112,80},{1... | collective-permute-start | bytes 2555912 | tf_op jit(solution)/shard_map/ppermute | solution.py:65
  107.4 0.7 collective-permute-start.18
  108.1 5.1 %collective-permute-done.5 = bf16[128,2048]{1,0:T(8,128)(2,1)S(1)} collective-permute-done((bf16[128,2048]{1,0:T(8,128)(2,1)S(1)}, bf16[128,2048]{1,0:T(8,128)(2,1)S(1)}, u32[]{:S(2)}, u32[]{:S(2)}) %collective-permute-start.5) | collective-permute-done | bytes 524320 | tf_op jit(solution)/shard_map/ppermute | solution.py:78
  113.2 1.6 collective-permute-start.14
  114.8 0.1 fusion.9
  114.9 3.8 %collective-permute-done.3 = bf16[128,2048]{1,0:T(8,128)(2,1)S(1)} collective-permute-done((bf16[128,2048]{1,0:T(8,128)(2,1)S(1)}, bf16[128,2048]{1,0:T(8,128)(2,1)S(1)}, u32[]{:S(2)}, u32[]{:S(2)}) %collective-permute-start.3) | collective-permute-done | bytes 524320 | tf_op jit(solution)/shard_map/ppermute | solution.py:77
  118.7 1.6 collective-permute-start.17
  120.3 0.1 fusion.10
  120.4 0.1 pad_maximum_fusion.1
  120.5 23.4 %collective-permute-done.18 = bf16[208,2048]{1,0:T(8,128)(2,1)S(1)} collective-permute-done((bf16[208,2048]{1,0:T(8,128)(2,1)S(1)}, bf16[208,2048]{1,0:T(8,128)(2,1)S(1)}, u32[]{:S(2)}, u32[]{:S(2)}) %collective-permute-start.18) | collective-permute-done | bytes 852000 | tf_op jit(solution)/shard_map/ppermute | solution.py:63
  143.9 0.6 fusion.6
  144.5 1.3 collective-permute-start.15
  145.9 2.7 %collective-permute-start.19 = (bf16[208,2048]{1,0:T(8,128)(2,1)S(1)}, bf16[208,2048]{1,0:T(8,128)(2,1)S(1)}, u32[]{:S(2)}, u32[]{:S(2)}) collective-permute-start(bf16[208,2048]{1,0:T(8,128)(2,1)S(1)} %get-tuple-element.7), channel_id=1, source_target_pairs={{0,96},{16,112},{32,0},{48,16},{64,32},{80,48},{96,64},{112,80},{1... | collective-permute-start | bytes 2555912 | tf_op jit(solution)/shard_map/ppermute | solution.py:67
  148.7 3.0 %collective-permute-start.6 = (bf16[256,2048]{1,0:T(8,128)(2,1)S(1)}, bf16[256,2048]{1,0:T(8,128)(2,1)S(1)}, u32[]{:S(2)}, u32[]{:S(2)}) collective-permute-start(bf16[256,2048]{1,0:T(8,128)(2,1)S(1)} %pad_maximum_fusion.1), channel_id=1, source_target_pairs={{0,12},{4,0},{8,4},{12,8},{1,13},{5,1},{9,5},{13,9},{2,14},{6,2},{... | collective-permute-start | bytes 3145736 | tf_op jit(solution)/shard_map/ppermute | solution.py:84
  151.7 0.2 fusion.8
  151.9 2.6 %collective-permute-done.17 = bf16[208,2048]{1,0:T(8,128)(2,1)S(1)} collective-permute-done((bf16[208,2048]{1,0:T(8,128)(2,1)S(1)}, bf16[208,2048]{1,0:T(8,128)(2,1)S(1)}, u32[]{:S(2)}, u32[]{:S(2)}) %collective-permute-start.17) | collective-permute-done | bytes 852000 | tf_op jit(solution)/shard_map/ppermute | solution.py:64
  154.6 5.2 %collective-permute-start.13 = (bf16[256,1664]{1,0:T(8,128)(2,1)S(1)}, bf16[256,1664]{1,0:T(8,128)(2,1)S(1)}, u32[]{:S(2)}, u32[]{:S(2)}) collective-permute-start(bf16[256,1664]{1,0:T(8,128)(2,1)S(1)} %fusion.8), channel_id=1, source_target_pairs={{0,0},{7,1},{10,2},{13,3},{1,4},{4,5},{11,6},{14,7},{2,8},{5,9},{8... | collective-permute-start | bytes 2555912 | tf_op jit(solution)/shard_map/ppermute | solution.py:96
  159.8 0.4 dynamic-slice_convert_fusion
  160.2 10.9 %collective-permute-done.15 = bf16[208,2048]{1,0:T(8,128)(2,1)S(1)} collective-permute-done((bf16[208,2048]{1,0:T(8,128)(2,1)S(1)}, bf16[208,2048]{1,0:T(8,128)(2,1)S(1)}, u32[]{:S(2)}, u32[]{:S(2)}) %collective-permute-start.15) | collective-permute-done | bytes 852000 | tf_op jit(solution)/shard_map/ppermute | solution.py:66
  171.1 0.8 select_convert_fusion
  172.0 2.2 %collective-permute-start.20 = (bf16[208,2048]{1,0:T(8,128)(2,1)S(1)}, bf16[208,2048]{1,0:T(8,128)(2,1)S(1)}, u32[]{:S(2)}, u32[]{:S(2)}) collective-permute-start(bf16[208,2048]{1,0:T(8,128)(2,1)S(1)} %select_convert_fusion), channel_id=1, source_target_pairs={{0,16},{16,0},{32,48},{48,32},{64,80},{80,64},{96,112},{112,96},{1... | collective-permute-start | bytes 2555912 | tf_op jit(solution)/shard_map/ppermute | solution.py:72
  174.2 19.0 %collective-permute-done.13 = bf16[256,1664]{1,0:T(8,128)(2,1)S(1)} collective-permute-done((bf16[256,1664]{1,0:T(8,128)(2,1)S(1)}, bf16[256,1664]{1,0:T(8,128)(2,1)S(1)}, u32[]{:S(2)}, u32[]{:S(2)}) %collective-permute-start.13) | collective-permute-done | bytes 852000 | tf_op jit(solution)/shard_map/ppermute | solution.py:96
  193.2 1.4 collective-permute-done.4
  194.6 3.2 %fusion.1 = bf16[256,2048]{1,0:T(8,128)(2,1)} fusion(bf16[1664,2048]{1,0:T(8,128)(2,1)S(1)} %bitcast.92, bf16[256,2048]{1,0:T(8,128)(2,1)S(1)} %collective-permute-done.6, bf16[256,2048]{1,0:T(8,128)(2,1)S(1)} %collective-permute-done.4, bf16[1024,1664]{1,0:T(8,128)(2,1)S(1)} %bitcast.80), kind=kOutput, calls=%fused_computation.5 | convolution fusion | flops 1747451904 | bytes 10813440 | tf_op jit(solution)/shard_map/dot_general | solution.py:22
  197.7 1.3 collective-permute-done.20
  199.0 2.1 %convert_add_fusion.3 = f32[208,2048]{1,0:T(8,128)} fusion(bf16[208,2048]{1,0:T(8,128)(2,1)S(1)} %collective-permute-done.20, pred[]{:T(512)S(6)} %eq.9, bf16[208,2048]{1,0:T(8,128)(2,1)S(1)} %collective-permute-done.16, bf16[208,2048]{1,0:T(8,128)(2,1)S(1)} %collective-permute-done.15, f32[1,416,2048]{2,1,0:T(8,128)S(1)} %dynamic-slice_convert_fusion, ...), kind=kLoop, calls=%fused_computation.21 | loop fusion | flops 4685824 | bytes 9371649 | tf_op jit(solution)/shard_map/add | solution.py:73
  201.2 0.9 copy.16
  (38 shorter events, 0.3 us)
Async XLA Ops:
  0.6 50.6 %copy-start.1 = (bf16[256,2048]{1,0:T(8,128)(2,1)S(1)}, bf16[256,2048]{1,0:T(8,128)(2,1)}, u32[]{:S(2)}) copy-start(bf16[256,2048]{1,0:T(8,128)(2,1)} %param.5) | copy-start | bytes 3145732
  0.6 45.7 %collective-permute-start.8 = (bf16[256,2048]{1,0:T(8,128)(2,1)}, bf16[256,2048]{1,0:T(8,128)(2,1)S(1)}, u32[]{:S(2)}, u32[]{:S(2)}) collective-permute-start(bf16[256,2048]{1,0:T(8,128)(2,1)} %param.5), channel_id=1, source_target_pairs={{0,4},{4,8},{8,12},{12,0},{1,5},{5,9},{9,13},{13,1},{2,6},{6,10},{... | collective-permute-start | bytes 3145736 | tf_op jit(solution)/shard_map/ppermute | solution.py:49
  2.6 44.6 %collective-permute-start.7 = (bf16[256,2048]{1,0:T(8,128)(2,1)}, bf16[256,2048]{1,0:T(8,128)(2,1)S(1)}, u32[]{:S(2)}, u32[]{:S(2)}) collective-permute-start(bf16[256,2048]{1,0:T(8,128)(2,1)} %param.5), channel_id=1, source_target_pairs={{0,12},{4,0},{8,4},{12,8},{1,13},{5,1},{9,5},{13,9},{2,14},{6,2},{... | collective-permute-start | bytes 3145736 | tf_op jit(solution)/shard_map/ppermute | solution.py:50
  4.8 47.5 %collective-permute-start = (bf16[256,1664]{1,0:T(8,128)(2,1)}, bf16[256,1664]{1,0:T(8,128)(2,1)S(1)}, u32[]{:S(2)}, u32[]{:S(2)}) collective-permute-start(bf16[256,1664]{1,0:T(8,128)(2,1)} %param.3), channel_id=1, source_target_pairs={{0,0},{1,7},{2,10},{3,13},{4,1},{5,4},{6,11},{7,14},{8,2},{9,5},{1... | collective-permute-start | bytes 2555912 | tf_op jit(solution)/shard_map/ppermute | solution.py:42
  47.2 14.5 %collective-permute-start.9 = (bf16[128,2048]{1,0:T(8,128)(2,1)}, bf16[128,2048]{1,0:T(8,128)(2,1)S(1)}, u32[]{:S(2)}, u32[]{:S(2)}) collective-permute-start(bf16[128,2048]{1,0:T(8,128)(2,1)} %slice.118), channel_id=1, source_target_pairs={{0,4},{4,8},{8,12},{12,0},{1,5},{5,9},{9,13},{13,1},{2,6},{6,10},{... | collective-permute-start | bytes 1572872 | tf_op jit(solution)/shard_map/ppermute | solution.py:51
  48.0 14.5 %collective-permute-start.10 = (bf16[128,2048]{1,0:T(8,128)(2,1)}, bf16[128,2048]{1,0:T(8,128)(2,1)}, u32[]{:S(2)}, u32[]{:S(2)}) collective-permute-start(bf16[128,2048]{1,0:T(8,128)(2,1)} %slice.119), channel_id=1, source_target_pairs={{0,12},{4,0},{8,4},{12,8},{1,13},{5,1},{9,5},{13,9},{2,14},{6,2},{... | collective-permute-start | bytes 1572872 | tf_op jit(solution)/shard_map/ppermute | solution.py:52
  52.3 22.2 %collective-permute-start.1 = (bf16[256,1664]{1,0:T(8,128)(2,1)S(1)}, bf16[256,1664]{1,0:T(8,128)(2,1)}, u32[]{:S(2)}, u32[]{:S(2)}) collective-permute-start(bf16[256,1664]{1,0:T(8,128)(2,1)S(1)} %collective-permute-done), channel_id=1, source_target_pairs={{0,2},{1,3},{2,0},{3,1},{4,6},{5,7},{6,4},{7,5},{8,10},{9,11},{10,... | collective-permute-start | bytes 2555912 | tf_op jit(solution)/shard_map/ppermute | solution.py:43
  61.7 7.1 %slice-start = ((s8[6815744]{0:T(1024)(128)(4,1)}), s8[4194304]{0:T(1024)(128)(4,1)S(1)}, s32[]{:S(2)}) async-start(s8[6815744]{0:T(1024)(128)(4,1)} %bitcast.85), calls=%async_computation | async-start | bytes 8388608
  66.1 3.0 %slice-start.1 = ((s8[6815744]{0:T(1024)(128)(4,1)}), s8[2621440]{0:T(1024)(128)(4,1)S(1)}, s32[]{:S(2)}) async-start(s8[6815744]{0:T(1024)(128)(4,1)} %bitcast.85), calls=%async_computation.1 | async-start | bytes 5242880
  74.3 3.9 %collective-permute-start.11 = (bf16[512,1664]{1,0:T(8,128)(2,1)}, bf16[512,1664]{1,0:T(8,128)(2,1)}, u32[]{:S(2)}, u32[]{:S(2)}) collective-permute-start(bf16[512,1664]{1,0:T(8,128)(2,1)} %convolution_convert_fusion), channel_id=1, source_target_pairs={{0,1},{1,0},{2,3},{3,2},{4,5},{5,4},{6,7},{7,6},{8,9},{9,8},{10,11... | collective-permute-start | bytes 5111816 | tf_op jit(solution)/shard_map/ppermute | solution.py:91
  75.8 10.3 %collective-permute-start.2 = (bf16[2,256,1664]{2,1,0:T(8,128)(2,1)S(1)}, bf16[2,256,1664]{2,1,0:T(8,128)(2,1)S(1)}, u32[]{:S(2)}, u32[]{:S(2)}) collective-permute-start(bf16[2,256,1664]{2,1,0:T(8,128)(2,1)S(1)} %bitcast_dynamic-update-slice_fusion.2), channel_id=1, source_target_pairs={{0,1},{1,0},{2,3},{3,2},{4,5},{5,4},{6,7},{7,6},{8,9},{9,8},{10,11... | collective-permute-start | bytes 5111816 | tf_op jit(solution)/shard_map/ppermute | solution.py:45
  76.6 9.8 %slice-start.2 = ((s8[6815744]{0:T(1024)(128)(4,1)}), s8[4194304]{0:T(1024)(128)(4,1)S(1)}, s32[]{:S(2)}) async-start(s8[6815744]{0:T(1024)(128)(4,1)} %bitcast.87), calls=%async_computation.2 | async-start | bytes 8388608
  78.2 8.2 %slice-start.3 = ((s8[6815744]{0:T(1024)(128)(4,1)}), s8[2621440]{0:T(1024)(128)(4,1)S(1)}, s32[]{:S(2)}) async-start(s8[6815744]{0:T(1024)(128)(4,1)} %bitcast.87), calls=%async_computation.3 | async-start | bytes 5242880
  85.9 62.8 %collective-permute-start.12 = (bf16[256,1664]{1,0:T(8,128)(2,1)S(1)}, bf16[256,1664]{1,0:T(8,128)(2,1)S(1)}, u32[]{:S(2)}, u32[]{:S(2)}) collective-permute-start(bf16[256,1664]{1,0:T(8,128)(2,1)S(1)} %fusion.11), channel_id=1, source_target_pairs={{0,2},{1,3},{2,0},{3,1},{4,6},{5,7},{6,4},{7,5},{8,10},{9,11},{10,... | collective-permute-start | bytes 2555912 | tf_op jit(solution)/shard_map/ppermute | solution.py:94
  86.2 2.4 %slice-start.4 = ((s8[6815744]{0:T(1024)(128)(4,1)}), s8[2621440]{0:T(1024)(128)(4,1)S(1)}, s32[]{:S(2)}) async-start(s8[6815744]{0:T(1024)(128)(4,1)} %bitcast.89), calls=%async_computation.4 | async-start | bytes 5242880
  86.5 2.8 %slice-start.5 = ((s8[6815744]{0:T(1024)(128)(4,1)}), s8[4194304]{0:T(1024)(128)(4,1)S(1)}, s32[]{:S(2)}) async-start(s8[6815744]{0:T(1024)(128)(4,1)} %bitcast.89), calls=%async_computation.5 | async-start | bytes 8388608
  89.2 2.2 %copy-start = (bf16[1024,2048]{1,0:T(8,128)(2,1)S(1)}, bf16[1024,2048]{1,0:T(8,128)(2,1)}, u32[]{:S(2)}) copy-start(bf16[1024,2048]{1,0:T(8,128)(2,1)} %constant_dynamic-update-slice_fusion) | copy-start | bytes 12582916
  89.2 12.5 %slice-start.6 = ((s8[6815744]{0:T(1024)(128)(4,1)}), s8[4194304]{0:T(1024)(128)(4,1)S(1)}, s32[]{:S(2)}) async-start(s8[6815744]{0:T(1024)(128)(4,1)} %bitcast.91), calls=%async_computation.6 | async-start | bytes 8388608
  91.4 10.3 %slice-start.7 = ((s8[6815744]{0:T(1024)(128)(4,1)}), s8[2621440]{0:T(1024)(128)(4,1)S(1)}, s32[]{:S(2)}) async-start(s8[6815744]{0:T(1024)(128)(4,1)} %bitcast.91), calls=%async_computation.7 | async-start | bytes 5242880
  99.2 14.0 %collective-permute-start.5 = (bf16[128,2048]{1,0:T(8,128)(2,1)S(1)}, bf16[128,2048]{1,0:T(8,128)(2,1)S(1)}, u32[]{:S(2)}, u32[]{:S(2)}) collective-permute-start(bf16[128,2048]{1,0:T(8,128)(2,1)S(1)} %get-tuple-element.12), channel_id=1, source_target_pairs={{0,12},{4,0},{8,4},{12,8},{1,13},{5,1},{9,5},{13,9},{2,14},{6,2},{... | collective-permute-start | bytes 1572872 | tf_op jit(solution)/shard_map/ppermute | solution.py:78
  103.8 15.0 %collective-permute-start.3 = (bf16[128,2048]{1,0:T(8,128)(2,1)S(1)}, bf16[128,2048]{1,0:T(8,128)(2,1)S(1)}, u32[]{:S(2)}, u32[]{:S(2)}) collective-permute-start(bf16[128,2048]{1,0:T(8,128)(2,1)S(1)} %get-tuple-element.11), channel_id=1, source_target_pairs={{0,4},{4,8},{8,12},{12,0},{1,5},{5,9},{9,13},{13,1},{2,6},{6,10},{... | collective-permute-start | bytes 1572872 | tf_op jit(solution)/shard_map/ppermute | solution.py:77
  104.3 47.5 %collective-permute-start.16 = (bf16[208,2048]{1,0:T(8,128)(2,1)S(1)}, bf16[208,2048]{1,0:T(8,128)(2,1)S(1)}, u32[]{:S(2)}, u32[]{:S(2)}) collective-permute-start(bf16[208,2048]{1,0:T(8,128)(2,1)S(1)} %get-tuple-element.4), channel_id=1, source_target_pairs={{0,96},{16,112},{32,0},{48,16},{64,32},{80,48},{96,64},{112,80},{1... | collective-permute-start | bytes 2555912 | tf_op jit(solution)/shard_map/ppermute | solution.py:65
  107.4 36.5 %collective-permute-start.18 = (bf16[208,2048]{1,0:T(8,128)(2,1)S(1)}, bf16[208,2048]{1,0:T(8,128)(2,1)S(1)}, u32[]{:S(2)}, u32[]{:S(2)}) collective-permute-start(bf16[208,2048]{1,0:T(8,128)(2,1)S(1)} %get-tuple-element.6), channel_id=1, source_target_pairs={{0,96},{16,112},{32,0},{48,16},{64,32},{80,48},{96,64},{112,80},{1... | collective-permute-start | bytes 2555912 | tf_op jit(solution)/shard_map/ppermute | solution.py:63
  113.2 30.7 %collective-permute-start.14 = (bf16[208,2048]{1,0:T(8,128)(2,1)S(1)}, bf16[208,2048]{1,0:T(8,128)(2,1)S(1)}, u32[]{:S(2)}, u32[]{:S(2)}) collective-permute-start(bf16[208,2048]{1,0:T(8,128)(2,1)S(1)} %get-tuple-element.5), channel_id=1, source_target_pairs={{0,32},{16,48},{32,64},{48,80},{64,96},{80,112},{96,0},{112,16},{1... | collective-permute-start | bytes 2555912 | tf_op jit(solution)/shard_map/ppermute | solution.py:62
  118.7 35.8 %collective-permute-start.17 = (bf16[208,2048]{1,0:T(8,128)(2,1)S(1)}, bf16[208,2048]{1,0:T(8,128)(2,1)S(1)}, u32[]{:S(2)}, u32[]{:S(2)}) collective-permute-start(bf16[208,2048]{1,0:T(8,128)(2,1)S(1)} %get-tuple-element.3), channel_id=1, source_target_pairs={{0,32},{16,48},{32,64},{48,80},{64,96},{80,112},{96,0},{112,16},{1... | collective-permute-start | bytes 2555912 | tf_op jit(solution)/shard_map/ppermute | solution.py:64
  144.5 26.6 %collective-permute-start.15 = (bf16[208,2048]{1,0:T(8,128)(2,1)S(1)}, bf16[208,2048]{1,0:T(8,128)(2,1)S(1)}, u32[]{:S(2)}, u32[]{:S(2)}) collective-permute-start(bf16[208,2048]{1,0:T(8,128)(2,1)S(1)} %get-tuple-element.8), channel_id=1, source_target_pairs={{0,32},{16,48},{32,64},{48,80},{64,96},{80,112},{96,0},{112,16},{1... | collective-permute-start | bytes 2555912 | tf_op jit(solution)/shard_map/ppermute | solution.py:66
  145.9 25.3 %collective-permute-start.19 = (bf16[208,2048]{1,0:T(8,128)(2,1)S(1)}, bf16[208,2048]{1,0:T(8,128)(2,1)S(1)}, u32[]{:S(2)}, u32[]{:S(2)}) collective-permute-start(bf16[208,2048]{1,0:T(8,128)(2,1)S(1)} %get-tuple-element.7), channel_id=1, source_target_pairs={{0,96},{16,112},{32,0},{48,16},{64,32},{80,48},{96,64},{112,80},{1... | collective-permute-start | bytes 2555912 | tf_op jit(solution)/shard_map/ppermute | solution.py:67
  148.7 44.5 %collective-permute-start.6 = (bf16[256,2048]{1,0:T(8,128)(2,1)S(1)}, bf16[256,2048]{1,0:T(8,128)(2,1)S(1)}, u32[]{:S(2)}, u32[]{:S(2)}) collective-permute-start(bf16[256,2048]{1,0:T(8,128)(2,1)S(1)} %pad_maximum_fusion.1), channel_id=1, source_target_pairs={{0,12},{4,0},{8,4},{12,8},{1,13},{5,1},{9,5},{13,9},{2,14},{6,2},{... | collective-permute-start | bytes 3145736 | tf_op jit(solution)/shard_map/ppermute | solution.py:84
  151.9 42.7 %collective-permute-start.4 = (bf16[256,2048]{1,0:T(8,128)(2,1)S(1)}, bf16[256,2048]{1,0:T(8,128)(2,1)S(1)}, u32[]{:S(2)}, u32[]{:S(2)}) collective-permute-start(bf16[256,2048]{1,0:T(8,128)(2,1)S(1)} %pad_maximum_fusion), channel_id=1, source_target_pairs={{0,4},{4,8},{8,12},{12,0},{1,5},{5,9},{9,13},{13,1},{2,6},{6,10},{... | collective-permute-start | bytes 3145736 | tf_op jit(solution)/shard_map/ppermute | solution.py:83
  154.6 38.6 %collective-permute-start.13 = (bf16[256,1664]{1,0:T(8,128)(2,1)S(1)}, bf16[256,1664]{1,0:T(8,128)(2,1)S(1)}, u32[]{:S(2)}, u32[]{:S(2)}) collective-permute-start(bf16[256,1664]{1,0:T(8,128)(2,1)S(1)} %fusion.8), channel_id=1, source_target_pairs={{0,0},{7,1},{10,2},{13,3},{1,4},{4,5},{11,6},{14,7},{2,8},{5,9},{8... | collective-permute-start | bytes 2555912 | tf_op jit(solution)/shard_map/ppermute | solution.py:96
  172.0 27.0 %collective-permute-start.20 = (bf16[208,2048]{1,0:T(8,128)(2,1)S(1)}, bf16[208,2048]{1,0:T(8,128)(2,1)S(1)}, u32[]{:S(2)}, u32[]{:S(2)}) collective-permute-start(bf16[208,2048]{1,0:T(8,128)(2,1)S(1)} %select_convert_fusion), channel_id=1, source_target_pairs={{0,16},{16,0},{32,48},{48,32},{64,80},{80,64},{96,112},{112,96},{1... | collective-permute-start | bytes 2555912 | tf_op jit(solution)/shard_map/ppermute | solution.py:72

commit v2 on v1

v2 whole, which is shorter than its diff:
```python
import math

import jax
import jax.numpy as jnp
from jax import lax
from jax.experimental import pallas as pl
from jax.experimental.pallas import tpu as pltpu
from jax.sharding import PartitionSpec as P

BF = jnp.bfloat16
F32 = jnp.float32
Z_UP = [(i, (i + 1) % 4) for i in range(4)]
Z_DOWN = [(i, (i + 3) % 4) for i in range(4)]
Y_UP = [(i, (i + 2) % 8) for i in range(8)]
Y_DOWN = [(i, (i + 6) % 8) for i in range(8)]
XHI = [(i, i ^ 1) for i in range(8)]
XLO = [(i, i ^ 2) for i in range(4)]
CORE = [(i, i ^ 1) for i in range(4)]
TO_PLANE = [(t * 4 + f, f * 4 + (t - f) % 4) for t in range(4) for f in range(4)]
TO_PLANE_X = [(a, b ^ 2) for a, b in TO_PLANE]
FROM_PLANE = [(b, a) for a, b in TO_PLANE]
FROM_PLANE_X = [(b, a) for a, b in TO_PLANE_X]
CHUNKS = ((0, 1024), (1024, 2048))


def dot(a, b, ca, cb):
    return lax.dot_general(a, b, (((ca,), (cb,)), ((), ())), preferred_element_type=F32)


def at(a, i):
    return lax.dynamic_index_in_dim(a, i, 0, keepdims=False)


def params(mib):
    return pltpu.CompilerParams(vmem_limit_bytes=mib * 1024 * 1024)


COST = pl.CostEstimate(flops=1000, bytes_accessed=1000, transcendentals=0)


def tokens_by_width(place, hs, w, block=256):
    def kernel(place_ref, *refs):
        w_ref, o_ref = refs[-2:]
        o = dot(jnp.concatenate([r[...] for r in refs[:-2]], axis=0), w_ref[...], 1, 0).astype(BF)
        rows = o_ref.shape[1]
        for k in range(4):
            o_ref[lax.rem(place_ref[0] + k, 4)] = o[k * rows : (k + 1) * rows]

    rows, n = hs[0].shape[0], w.shape[1]
    return pl.pallas_call(
        kernel,
        grid_spec=pltpu.PrefetchScalarGridSpec(
            num_scalar_prefetch=1,
            grid=(n // block,),
            in_specs=[pl.BlockSpec(h.shape, lambda i, p: (0, 0), pipeline_mode=pl.Buffered(1)) for h in hs]
            + [pl.BlockSpec((w.shape[0], block), lambda i, p: (0, i))],
            out_specs=pl.BlockSpec((4, rows, block), lambda i, p: (0, 0, i)),
        ),
        out_shape=jax.ShapeDtypeStruct((4, rows, n), BF),
        cost_estimate=COST,
        compiler_params=params(16),
    )(place, *hs, w)


def after(token, *values):
    return lax.optimization_barrier((token,) + values)[1:]


def shards(hidden, weight, upstream):
    z, d, c = lax.axis_index("row"), lax.axis_index("dp"), lax.axis_index("col")
    y, xhi, xlo, core = d // 2, d % 2, c // 2, c % 2
    rows, f = hidden.shape
    half = rows // 2
    left, even, low = xlo == 0, core == 0, xhi == 0

    own_a = lax.ppermute(hidden[:half], ("row", "col"), TO_PLANE)
    own_b = lax.ppermute(hidden[half:], ("row", "col"), TO_PLANE_X)
    u3 = lax.ppermute(upstream, "row", Z_UP)
    u1 = lax.ppermute(upstream, "row", Z_DOWN)
    g0 = dot(upstream, weight, 1, 1).astype(BF)
    own = jnp.stack([own_a, own_b])
    swapped = lax.ppermute(own, "col", XLO)
    two = jnp.stack(
        [
            jnp.where(left, own_a, swapped[0]),
            jnp.where(left, swapped[1], own_b),
            jnp.where(left, swapped[0], own_a),
            jnp.where(left, own_b, swapped[1]),
        ]
    ).reshape(2, rows, f)
    other = lax.ppermute(two, "col", CORE)
    hs = (
        jnp.where(even, two[0], other[0]),
        jnp.where(even, other[0], two[0]),
        jnp.where(even, two[1], other[1]),
        jnp.where(even, other[1], two[1]),
    )

    u2a = lax.ppermute(u3[:half], "row", Z_UP)
    u2b = lax.ppermute(u1[half:], "row", Z_DOWN)
    g1, g3 = dot(u1, weight, 1, 1).astype(BF), dot(u3, weight, 1, 1).astype(BF)

    o = tokens_by_width(jnp.reshape(z, (1,)).astype(jnp.int32), hs, weight)
    o_in = lax.all_to_all(o, "row", 0, 0, tiled=True)

    u2a, u2b = after(o, u2a, u2b)
    g2 = dot(jnp.concatenate([u2a, u2b], axis=0), weight, 1, 1).astype(BF)
    g_send = jnp.stack([jnp.where(even, g1, g0), jnp.where(even, g3, g2)])
    g_in = lax.ppermute(g_send, "col", CORE)
    hs = after(g_send, *hs)

    token_count = lax.axis_size("dp") * lax.axis_size("row") * rows
    factor = 1.0 / math.sqrt(token_count)
    hf = f // 8
    near, was, wbs = [], [], []
    u = jnp.concatenate([upstream, u1, u2a, u2b, u3], axis=0)
    for lo, hi in CHUNKS:
        wg = (dot(jnp.concatenate(hs, axis=0), u[:, lo:hi], 0, 0) * factor).astype(BF)
        wg = wg.reshape(4, f // 4, hi - lo)
        w2 = at(wg, (y + 2) % 4)
        w2a, w2b = w2[:hf], w2[hf:]
        rest = [at(wg, (y + 1) % 4), at(wg, (y + 3) % 4), at(wg, y)]
        hs = after(w2a, *hs)
        was.append(lax.ppermute(w2a, "dp", Y_UP))
        wbs.append(lax.ppermute(w2b, "dp", Y_DOWN))
        near.append(rest)

    def second(i):
        w1, w3, _ = near[i]
        w1 = lax.dynamic_update_slice(w1, (w1[:hf].astype(F32) + was[i].astype(F32)).astype(BF), (0, 0))
        w3 = lax.dynamic_update_slice(w3, (w3[hf:].astype(F32) + wbs[i].astype(F32)).astype(BF), (hf, 0))
        w1, w3 = lax.optimization_barrier((w1, w3))
        return w1, w3, lax.ppermute(w1, "dp", Y_UP), lax.ppermute(w3, "dp", Y_DOWN)

    was[0], wbs[0] = after(w2a, was[0], wbs[0])
    w1, w3, s1, s3 = second(0)

    (g_in,) = after(w3, g_in)
    g0 = jnp.where(even, g0, g1).astype(F32) + g_in[0].astype(F32)
    g1 = jnp.where(even, g2, g3).astype(F32) + g_in[1].astype(F32)
    keep_a, keep_b = jnp.where(left, g0[:half], g1[:half]), jnp.where(left, g1[half:], g0[half:])
    send = jnp.stack([jnp.where(left, g1[:half], g0[:half]), jnp.where(left, g0[half:], g1[half:])])
    send = send.astype(BF)
    g_x = lax.ppermute(send, "col", XLO)

    was[1], wbs[1] = after(send, was[1], wbs[1])
    w1, w3, v1, v3 = second(1)

    def over_x(i, s1, s3):
        t = near[i][2].astype(F32) + s1.astype(F32) + s3.astype(F32)
        out = jnp.where(low, t[hf:], t[:hf]).astype(BF)
        return out, jnp.where(low, t[:hf], t[hf:]), lax.ppermute(out, "dp", XHI)

    s1, s3 = after(w3, s1, s3)
    x_out, mine0, x0 = over_x(0, s1, s3)

    (g_x,) = after(x_out, g_x)
    g_a, g_b = (keep_a + g_x[0].astype(F32)).astype(BF), (keep_b + g_x[1].astype(F32)).astype(BF)
    h_a = lax.ppermute(g_a, ("row", "col"), FROM_PLANE)
    h_b = lax.ppermute(g_b, ("row", "col"), FROM_PLANE_X)

    v1, v3 = after(g_b, v1, v3)
    x_out, mine1, x1 = over_x(1, v1, v3)

    (o_in,) = after(x_out, o_in)
    output = jnp.sum(o_in.astype(F32), axis=0).astype(BF)

    weight_grad = jnp.concatenate([mine0 + x0.astype(F32), mine1 + x1.astype(F32)], axis=1)
    hidden_grad = jnp.concatenate([h_a, h_b], axis=0)
    return (output, hidden_grad, weight_grad)


def solution(mesh):
    return jax.shard_map(
        shards,
        mesh=mesh,
        in_specs=(P(("dp", "row"), "col"), P("row", "col"), P(("dp", "row"), "col")),
        out_specs=(P(("dp", "row"), "col"), P(("dp", "row"), "col"), P(("row", "dp"), "col")),
        check_vma=False,
    )
```

time: 203 us -> 177 us (0.87)
  waiting for transfers between devices: 115 us -> 61.8 us
  starting transfers between devices: 36.1 us -> 56.8 us
  Pallas kernels: 0 us -> 10.6 us
  other arithmetic: 4.59 us -> 14.8 us
  matrix products: 29.7 us -> 22.7 us
  local copies, waits for them, and re-layouts: 15.7 us -> 8.78 us
    ppermute x1, waiting for transfers between devices: 37.9 us -> 11.1 us  [shards(): u3 = lax.ppermute(upstream, 'row', Z_UP)]
    ppermute x16 -> x17, waiting for transfers between devices: 67.5 us -> 50.7 us  [the longest x2 24.5 us: second(): lax.ppermute(w1, 'dp', Y_UP)]
    ppermute x16 -> x17, starting transfers between devices: 28.7 us -> 44.8 us  [the longest x1 6.63 us: shards(): h_a = lax.ppermute(g_a, ('row', 'col'), FROM_PLANE)]
    pallas_call x0 -> x1, Pallas kernels: none -> 10.6 us  [tokens_by_width(): pl.pallas_call(kernel, grid_spec=pltpu.PrefetchScalarGridSpec(num_scalar_...]
    ppermute x1, waiting for transfers between devices: 8.34 us -> 0.01 us  [shards(): u2a = lax.ppermute(u3[:half], 'row', Z_UP)]
    dot_general x7 -> x6, matrix products: 29.7 us -> 22.7 us  [dot(): lax.dot_general(a, b, (((ca,), (cb,)), ((), ())), preferred_element_type=...]
    all_to_all x0 -> x1, starting transfers between devices: none -> 4.86 us  [shards(): o_in = lax.all_to_all(o, 'row', 0, 0, tiled=True)]
    reduce_sum x0 -> x1, other arithmetic: none -> 4.25 us  [shards(): output = jnp.sum(o_in.astype(F32), axis=0).astype(BF)]
  transfers between devices with their start and end apart: 21 -> 23, of which waited for: 11 -> 8; matrix products, arithmetic and copies ran while one was open for 23% -> 19% of each run, Pallas kernels for 0% -> 6%
where the time goes in v2:
time: 177 us
  waiting for transfers between devices  61.8 us (35%)
  starting transfers between devices  56.8 us (32%)
  matrix products  22.7 us (13%)
  other arithmetic  14.8 us (8%)
  Pallas kernels  10.6 us (6%)
  local copies, waits for them, and re-layouts  8.78 us (5%)
    ppermute x2, waiting for transfers between devices, second(): lax.ppermute(w1, 'dp', Y_UP)  24.5 us
    dot_general x6, matrix products, dot(): lax.dot_general(a, b, (((ca,), (cb,)), ((), ())), preferred_element_type=...  22.7 us
    ppermute x1, waiting for transfers between devices, shards(): u3 = lax.ppermute(upstream, 'row', Z_UP)  11.1 us
    pallas_call x1, Pallas kernels, tokens_by_width(): pl.pallas_call(kernel, grid_spec=pltpu.PrefetchScalarGridSpec(num_scalar_...  10.6 us
    ppermute x2, waiting for transfers between devices, over_x(): return (out, jnp.where(low, t[:hf], t[hf:]), lax.ppermute(out, 'dp', XHI))  9.9 us
    ppermute x1, waiting for transfers between devices, shards(): h_a = lax.ppermute(g_a, ('row', 'col'), FROM_PLANE)  7.21 us
    ppermute x1, waiting for transfers between devices, shards(): own_a = lax.ppermute(hidden[:half], ('row', 'col'), TO_PLANE)  7 us
    ppermute x1, starting transfers between devices, shards(): h_a = lax.ppermute(g_a, ('row', 'col'), FROM_PLANE)  6.63 us
  transfers between devices with their start and end apart: 23, of which 8 were waited for; matrix products, arithmetic and copies ran while one was open for 19% of the time, Pallas kernels for 6%

profile of v2, /device:TPU:2, one launch (start us, length us, event | category | flops | bytes accessed | tf_op | source)
XLA Modules:
  0.0 176.7 jit_solution(6186039392908951111)
XLA Ops:
  0.6 2.0 %fusion.36 = (bf16[128,1664]{1,0:T(8,128)(2,1)}, bf16[128,1664]{1,0:T(8,128)(2,1)S(1)}) fusion(bf16[256,1664]{1,0:T(8,128)(2,1)} %param.3), kind=kLoop, calls=%fused_computation.97 | loop fusion | bytes 1703936 | tf_op jit(solution)/shard_map/slice | solution.py:76
  2.6 5.8 %collective-permute-start.2 = (bf16[128,1664]{1,0:T(8,128)(2,1)}, bf16[128,1664]{1,0:T(8,128)(2,1)S(1)}, u32[]{:S(2)}, u32[]{:S(2)}) collective-permute-start(bf16[128,1664]{1,0:T(8,128)(2,1)} %get-tuple-element.83), channel_id=1, source_target_pairs={{0,0},{1,7},{2,10},{3,13},{4,1},{5,4},{6,11},{7,14},{8,2},{9,5},{1... | collective-permute-start | bytes 1277960 | tf_op jit(solution)/shard_map/ppermute | solution.py:76
  8.4 2.5 %collective-permute-start.3 = (bf16[128,1664]{1,0:T(8,128)(2,1)S(1)}, bf16[128,1664]{1,0:T(8,128)(2,1)S(1)}, u32[]{:S(2)}, u32[]{:S(2)}) collective-permute-start(bf16[128,1664]{1,0:T(8,128)(2,1)S(1)} %get-tuple-element.84), channel_id=1, source_target_pairs={{0,2},{1,5},{2,8},{3,15},{4,3},{5,6},{6,9},{7,12},{8,0},{9,7},{10,... | collective-permute-start | bytes 1277960 | tf_op jit(solution)/shard_map/ppermute | solution.py:77
  10.9 3.2 %collective-permute-start = (bf16[256,2048]{1,0:T(8,128)(2,1)}, bf16[256,2048]{1,0:T(8,128)(2,1)S(1)}, u32[]{:S(2)}, u32[]{:S(2)}) collective-permute-start(bf16[256,2048]{1,0:T(8,128)(2,1)} %param.5), channel_id=1, source_target_pairs={{0,12},{4,0},{8,4},{12,8},{1,13},{5,1},{9,5},{13,9},{2,14},{6,2},{... | collective-permute-start | bytes 3145736 | tf_op jit(solution)/shard_map/ppermute | solution.py:79
  14.1 7.0 %collective-permute-done.2 = bf16[128,1664]{1,0:T(8,128)(2,1)S(1)} collective-permute-done((bf16[128,1664]{1,0:T(8,128)(2,1)}, bf16[128,1664]{1,0:T(8,128)(2,1)S(1)}, u32[]{:S(2)}, u32[]{:S(2)}) %collective-permute-start.2) | collective-permute-done | bytes 426016 | tf_op jit(solution)/shard_map/ppermute | solution.py:76
  21.2 2.8 %collective-permute-start.4 = (bf16[2,128,1664]{2,1,0:T(8,128)(2,1)S(1)}, bf16[2,128,1664]{2,1,0:T(8,128)(2,1)S(1)}, u32[]{:S(2)}, u32[]{:S(2)}) collective-permute-start(bf16[2,128,1664]{2,1,0:T(8,128)(2,1)S(1)} %pad_maximum_fusion.3), channel_id=1, source_target_pairs={{0,2},{1,3},{2,0},{3,1},{4,6},{5,7},{6,4},{7,5},{8,10},{9,11},{10,... | collective-permute-start | bytes 2555912 | tf_op jit(solution)/shard_map/ppermute | solution.py:82
  24.0 1.5 constant_dynamic-update-slice_fusion.4
  25.6 5.2 %convolution_convert_fusion.2 = bf16[256,1664]{1,0:T(8,128)(2,1)S(1)} fusion(bf16[256,2048]{1,0:T(8,128)(2,1)S(1)} %copy-done.13, bf16[1664,2048]{1,0:T(8,128)(2,1)} %refs_4_.1), kind=kOutput, calls=%fused_computation.18 | convolution fusion | flops 1745256448 | bytes 8716288 | tf_op jit(solution)/shard_map/dot_general | solution.py:27
  30.8 11.1 %collective-permute-done.1 = bf16[256,2048]{1,0:T(8,128)(2,1)S(1)} collective-permute-done((bf16[256,2048]{1,0:T(8,128)(2,1)}, bf16[256,2048]{1,0:T(8,128)(2,1)S(1)}, u32[]{:S(2)}, u32[]{:S(2)}) %collective-permute-start.1) | collective-permute-done | bytes 1048608 | tf_op jit(solution)/shard_map/ppermute | solution.py:78
  42.0 3.3 %collective-permute-start.7 = (bf16[128,2048]{1,0:T(8,128)(2,1)S(1)}, bf16[128,2048]{1,0:T(8,128)(2,1)S(1)}, u32[]{:S(2)}, u32[]{:S(2)}) collective-permute-start(bf16[128,2048]{1,0:T(8,128)(2,1)S(1)} %slice.165), channel_id=1, source_target_pairs={{0,12},{4,0},{8,4},{12,8},{1,13},{5,1},{9,5},{13,9},{2,14},{6,2},{... | collective-permute-start | bytes 1572872 | tf_op jit(solution)/shard_map/ppermute | solution.py:100
  45.3 0.2 select_bitcast_fusion.3
  45.5 0.3 pad_maximum_fusion
  45.7 0.3 collective-permute-start.5
  46.0 2.1 %convolution_convert_fusion.3 = bf16[256,1664]{1,0:T(8,128)(2,1)S(1)} fusion(bf16[256,2048]{1,0:T(8,128)(2,1)S(1)} %collective-permute-done, bf16[1664,2048]{1,0:T(8,128)(2,1)S(1)} %bitcast.114), kind=kOutput, calls=%fused_computation.19 | convolution fusion | flops 1745256448 | bytes 8716288 | tf_op jit(solution)/shard_map/dot_general | solution.py:27
  48.3 0.1 select_bitcast_fusion.1
  48.4 2.1 %convolution_convert_fusion.1 = bf16[256,1664]{1,0:T(8,128)(2,1)S(1)} fusion(bf16[256,2048]{1,0:T(8,128)(2,1)S(1)} %collective-permute-done.1, bf16[1664,2048]{1,0:T(8,128)(2,1)S(1)} %bitcast.114), kind=kOutput, calls=%fused_computation.17 | convolution fusion | flops 1745256448 | bytes 8716288 | tf_op jit(solution)/shard_map/dot_general | solution.py:27
  50.5 0.2 pad_maximum_fusion.4
  50.7 0.5 bitcast_select_fusion
  51.2 10.6 %shard_map.58 = bf16[4,256,2048]{2,1,0:T(8,128)(2,1)S(1)} custom-call(s32[1]{0:T(128)} %bitcast.1.place_ref, bf16[256,1664]{1,0:T(8,128)(2,1)S(1)} %get-tuple-element.34.refs_0_, bf16[256,1664]{1,0:T(8,128)(2,1)S(1)} %get-tuple-element.35.refs_1_, bf16[256,1664]{1,0:T(8,128)(2,1)S(1)} %get-tuple-element.36.refs_2_, ...), custom_call_target="tpu_custom_call" | custom-call | flops 1000 | bytes 1000 | tf_op jit(solution)/shard_map/pallas_call | solution.py:50
  61.7 2.0 %copy-done = bf16[4,256,2048]{2,1,0:T(8,128)(2,1)} copy-done((bf16[4,256,2048]{2,1,0:T(8,128)(2,1)}, bf16[4,256,2048]{2,1,0:T(8,128)(2,1)S(1)}, u32[]{:S(2)}) %copy-start) | copy-done | bytes 4194328
  63.7 2.1 %convolution_convert_fusion = bf16[256,1664]{1,0:T(8,128)(2,1)S(1)} fusion(bf16[1664,2048]{1,0:T(8,128)(2,1)S(1)} %bitcast.114, bf16[128,2048]{1,0:T(8,128)(2,1)S(1)} %collective-permute-done.7, bf16[128,2048]{1,0:T(8,128)(2,1)S(1)} %collective-permute-done.6), kind=kOutput, calls=%fused_computation.16 | convolution fusion | flops 1747353600 | bytes 8716288 | tf_op jit(solution)/shard_map/dot_general | solution.py:27
  65.9 0.1 select_bitcast_fusion
  66.0 1.4 pad_maximum_fusion.1
  67.3 0.5 collective-permute-start.10
  67.9 0.1 constant_dynamic-update-slice_fusion
  68.0 4.8 %multiply_convert_fusion.1 = bf16[1664,1024]{1,0:T(8,128)(2,1)S(1)} fusion(bf16[256,1664]{1,0:T(8,128)(2,1)S(1)} %get-tuple-element.37.refs_3_, bf16[256,1664]{1,0:T(8,128)(2,1)S(1)} %get-tuple-element.36.refs_2_, bf16[256,1664]{1,0:T(8,128)(2,1)S(1)} %get-tuple-element.35.refs_1_, bf16[256,1664]{1,0:T(8,128)(2,1)S(1)} %get-tuple-element.34.refs_0_, ...), kind=kOutput, calls=%fused_computation.1 | convolution fusion | flops 3506700288 | bytes 8912896 | tf_op jit(solution)/shard_map/dot_general | solution.py:27
  72.9 1.7 copy-done.1
  74.6 1.0 dynamic-slice_bitcast_fusion.8
  75.6 1.6 collective-permute-start.8
  77.1 4.9 %all-to-all-start = ((bf16[4,256,2048]{2,1,0:T(8,128)(2,1)}), bf16[4,256,2048]{2,1,0:T(8,128)(2,1)}, u32[]{:S(2)}, u32[]{:S(2)}) async-start(bf16[4,256,2048]{2,1,0:T(8,128)(2,1)} %copy-done), calls=%async_computation | async-start | bytes 8388608 | tf_op jit(solution)/shard_map/all_to_all | solution.py:104
  82.0 2.0 %collective-permute-start.9 = (bf16[208,1024]{1,0:T(8,128)(2,1)}, bf16[208,1024]{1,0:T(8,128)(2,1)S(1)}, u32[]{:S(2)}, u32[]{:S(2)}) collective-permute-start(bf16[208,1024]{1,0:T(8,128)(2,1)} %get-tuple-element.67), channel_id=1, source_target_pairs={{0,96},{16,112},{32,0},{48,16},{64,32},{80,48},{96,64},{112,80},{1... | collective-permute-start | bytes 1277960 | tf_op jit(solution)/shard_map/ppermute | solution.py:125
  84.0 6.4 %multiply_convert_fusion = bf16[1664,1024]{1,0:T(8,128)(2,1)S(1)} fusion(bf16[256,1664]{1,0:T(8,128)(2,1)S(1)} %get-tuple-element.37.refs_3_, bf16[256,1664]{1,0:T(8,128)(2,1)S(1)} %get-tuple-element.36.refs_2_, bf16[256,1664]{1,0:T(8,128)(2,1)S(1)} %get-tuple-element.35.refs_1_, bf16[256,1664]{1,0:T(8,128)(2,1)S(1)} %get-tuple-element.34.refs_0_, ...), kind=kOutput, calls=%fused_computation | convolution fusion | flops 3506700288 | bytes 8912896 | tf_op jit(solution)/shard_map/dot_general | solution.py:27
  90.5 0.7 collective-permute-start.11
  91.2 2.6 %collective-permute-start.12 = (bf16[208,1024]{1,0:T(8,128)(2,1)S(1)}, bf16[208,1024]{1,0:T(8,128)(2,1)S(1)}, u32[]{:S(2)}, u32[]{:S(2)}) collective-permute-start(bf16[208,1024]{1,0:T(8,128)(2,1)S(1)} %get-tuple-element.59), channel_id=1, source_target_pairs={{0,96},{16,112},{32,0},{48,16},{64,32},{80,48},{96,64},{112,80},{1... | collective-permute-start | bytes 1277960 | tf_op jit(solution)/shard_map/ppermute | solution.py:125
  93.8 0.1 dynamic-slice_bitcast_fusion.2
  93.9 1.2 collective-permute-done.9
  95.2 1.3 fusion.30
  96.5 1.7 collective-permute-start.13
  98.2 1.7 collective-permute-start.14
  99.8 2.0 %convert_add_fusion.2 = (f32[256,1664]{1,0:T(8,128)S(1)}, f32[256,1664]{1,0:T(8,128)S(1)}) fusion(bf16[2,256,1664]{2,1,0:T(8,128)(2,1)} %collective-permute-done.10, bf16[256,1664]{1,0:T(8,128)(2,1)S(1)} %copy-done.10, bf16[256,1664]{1,0:T(8,128)(2,1)S(1)} %copy-done.8, pred[]{:T(512)S(6)} %eq.19, bf16[256,1664]{1,0:T(8,128)(2,1)S(1)} %copy-done.4, ...), kind=kLoop, calls=%fused_computation.28 | loop fusion | flops 3407872 | bytes 8519681 | tf_op jit(solution)/shard_map/add | solution.py:140
  101.8 0.2 fusion.27
  102.0 0.1 pad_maximum_fusion.6
  102.1 2.8 %collective-permute-start.15 = (bf16[2,128,1664]{2,1,0:T(8,128)(2,1)S(1)}, bf16[2,128,1664]{2,1,0:T(8,128)(2,1)S(1)}, u32[]{:S(2)}, u32[]{:S(2)}) collective-permute-start(bf16[2,128,1664]{2,1,0:T(8,128)(2,1)S(1)} %pad_maximum_fusion.6), channel_id=1, source_target_pairs={{0,2},{1,3},{2,0},{3,1},{4,6},{5,7},{6,4},{7,5},{8,10},{9,11},{10,... | collective-permute-start | bytes 2555912 | tf_op jit(solution)/shard_map/ppermute | solution.py:144
  104.9 0.1 dynamic-slice_bitcast_fusion
  105.0 0.3 fusion.32
  105.4 2.8 %collective-permute-start.17 = (bf16[416,1024]{1,0:T(8,128)(2,1)S(1)}, bf16[416,1024]{1,0:T(8,128)(2,1)S(1)}, u32[]{:S(2)}, u32[]{:S(2)}) collective-permute-start(bf16[416,1024]{1,0:T(8,128)(2,1)S(1)} %get-tuple-element.44), channel_id=1, source_target_pairs={{0,96},{16,112},{32,0},{48,16},{64,32},{80,48},{96,64},{112,80},{1... | collective-permute-start | bytes 2555912 | tf_op jit(solution)/shard_map/ppermute | solution.py:133
  108.1 13.5 %collective-permute-done.13 = bf16[416,1024]{1,0:T(8,128)(2,1)S(1)} collective-permute-done((bf16[416,1024]{1,0:T(8,128)(2,1)S(1)}, bf16[416,1024]{1,0:T(8,128)(2,1)S(1)}, u32[]{:S(2)}, u32[]{:S(2)}) %collective-permute-start.13) | collective-permute-done | bytes 852000 | tf_op jit(solution)/shard_map/ppermute | solution.py:133
  121.7 0.9 collective-permute-done.14
  122.6 1.6 collective-permute-start.16
  124.1 0.4 fusion.16
  124.7 2.5 %collective-permute-start.20 = (bf16[208,1024]{1,0:T(8,128)(2,1)S(1)}, bf16[208,1024]{1,0:T(8,128)(2,1)S(1)}, u32[]{:S(2)}, u32[]{:S(2)}) collective-permute-start(bf16[208,1024]{1,0:T(8,128)(2,1)S(1)} %select_convert_fusion.1), channel_id=1, source_target_pairs={{0,16},{16,0},{32,48},{48,32},{64,80},{80,64},{96,112},{112,96},{1... | collective-permute-start | bytes 1277960 | tf_op jit(solution)/shard_map/ppermute | solution.py:152
  127.2 0.2 fusion.21
  127.4 4.9 %collective-permute-start.19 = (bf16[128,1664]{1,0:T(8,128)(2,1)S(1)}, bf16[128,1664]{1,0:T(8,128)(2,1)S(1)}, u32[]{:S(2)}, u32[]{:S(2)}) collective-permute-start(bf16[128,1664]{1,0:T(8,128)(2,1)S(1)} %get-tuple-element.54), channel_id=1, source_target_pairs={{2,0},{5,1},{8,2},{15,3},{3,4},{6,5},{9,6},{12,7},{0,8},{7,9},{10,... | collective-permute-start | bytes 1277960 | tf_op jit(solution)/shard_map/ppermute | solution.py:160
  132.3 10.9 %collective-permute-done.16 = bf16[416,1024]{1,0:T(8,128)(2,1)S(1)} collective-permute-done((bf16[416,1024]{1,0:T(8,128)(2,1)S(1)}, bf16[416,1024]{1,0:T(8,128)(2,1)S(1)}, u32[]{:S(2)}, u32[]{:S(2)}) %collective-permute-start.16) | collective-permute-done | bytes 852000 | tf_op jit(solution)/shard_map/ppermute | solution.py:133
  143.3 6.6 %collective-permute-start.18 = (bf16[128,1664]{1,0:T(8,128)(2,1)S(1)}, bf16[128,1664]{1,0:T(8,128)(2,1)S(1)}, u32[]{:S(2)}, u32[]{:S(2)}) collective-permute-start(bf16[128,1664]{1,0:T(8,128)(2,1)S(1)} %get-tuple-element.53), channel_id=1, source_target_pairs={{0,0},{7,1},{10,2},{13,3},{1,4},{4,5},{11,6},{14,7},{2,8},{5,9},{8... | collective-permute-start | bytes 1277960 | tf_op jit(solution)/shard_map/ppermute | solution.py:159
  149.9 0.4 fusion.17
  150.4 2.2 %collective-permute-start.21 = (bf16[208,1024]{1,0:T(8,128)(2,1)S(1)}, bf16[208,1024]{1,0:T(8,128)(2,1)S(1)}, u32[]{:S(2)}, u32[]{:S(2)}) collective-permute-start(bf16[208,1024]{1,0:T(8,128)(2,1)S(1)} %select_convert_fusion), channel_id=1, source_target_pairs={{0,16},{16,0},{32,48},{48,32},{64,80},{80,64},{96,112},{112,96},{1... | collective-permute-start | bytes 1277960 | tf_op jit(solution)/shard_map/ppermute | solution.py:152
  152.6 0.2 convert_add_fusion.11
  152.8 7.2 %collective-permute-done.18 = bf16[128,1664]{1,0:T(8,128)(2,1)S(1)} collective-permute-done((bf16[128,1664]{1,0:T(8,128)(2,1)S(1)}, bf16[128,1664]{1,0:T(8,128)(2,1)S(1)}, u32[]{:S(2)}, u32[]{:S(2)}) %collective-permute-start.18) | collective-permute-done | bytes 426016 | tf_op jit(solution)/shard_map/ppermute | solution.py:159
  160.1 1.0 pad_maximum_fusion.7
  161.0 9.9 %collective-permute-done.21 = bf16[208,1024]{1,0:T(8,128)(2,1)S(1)} collective-permute-done((bf16[208,1024]{1,0:T(8,128)(2,1)S(1)}, bf16[208,1024]{1,0:T(8,128)(2,1)S(1)}, u32[]{:S(2)}, u32[]{:S(2)}) %collective-permute-start.21) | collective-permute-done | bytes 426016 | tf_op jit(solution)/shard_map/ppermute | solution.py:152
  170.9 0.2 convert_add_fusion.10
  171.1 1.3 pad_maximum_fusion.2
  172.4 4.2 %reduce_sum.12 = bf16[256,2048]{1,0:T(8,128)(2,1)} reduce(bf16[4,256,2048]{2,1,0:T(8,128)(2,1)} %all-to-all-done, bf16[]{:T(256)} %constant.99.clone.1), dimensions={0}, to_apply=%region_0.1 | reduce | flops 1572864 | bytes 5242882 | tf_op jit(solution)/shard_map/reduce_sum | solution.py:166
  (59 shorter events, 0.8 us)
Async XLA Ops:
  2.6 18.6 %collective-permute-start.2 = (bf16[128,1664]{1,0:T(8,128)(2,1)}, bf16[128,1664]{1,0:T(8,128)(2,1)S(1)}, u32[]{:S(2)}, u32[]{:S(2)}) collective-permute-start(bf16[128,1664]{1,0:T(8,128)(2,1)} %get-tuple-element.83), channel_id=1, source_target_pairs={{0,0},{1,7},{2,10},{3,13},{4,1},{5,4},{6,11},{7,14},{8,2},{9,5},{1... | collective-permute-start | bytes 1277960 | tf_op jit(solution)/shard_map/ppermute | solution.py:76
  8.4 12.8 %collective-permute-start.3 = (bf16[128,1664]{1,0:T(8,128)(2,1)S(1)}, bf16[128,1664]{1,0:T(8,128)(2,1)S(1)}, u32[]{:S(2)}, u32[]{:S(2)}) collective-permute-start(bf16[128,1664]{1,0:T(8,128)(2,1)S(1)} %get-tuple-element.84), channel_id=1, source_target_pairs={{0,2},{1,5},{2,8},{3,15},{4,3},{5,6},{6,9},{7,12},{8,0},{9,7},{10,... | collective-permute-start | bytes 1277960 | tf_op jit(solution)/shard_map/ppermute | solution.py:77
  10.8 31.0 %collective-permute-start.1 = (bf16[256,2048]{1,0:T(8,128)(2,1)}, bf16[256,2048]{1,0:T(8,128)(2,1)S(1)}, u32[]{:S(2)}, u32[]{:S(2)}) collective-permute-start(bf16[256,2048]{1,0:T(8,128)(2,1)} %param.5), channel_id=1, source_target_pairs={{0,4},{4,8},{8,12},{12,0},{1,5},{5,9},{9,13},{13,1},{2,6},{6,10},{... | collective-permute-start | bytes 3145736 | tf_op jit(solution)/shard_map/ppermute | solution.py:78
  10.9 31.0 %collective-permute-start = (bf16[256,2048]{1,0:T(8,128)(2,1)}, bf16[256,2048]{1,0:T(8,128)(2,1)S(1)}, u32[]{:S(2)}, u32[]{:S(2)}) collective-permute-start(bf16[256,2048]{1,0:T(8,128)(2,1)} %param.5), channel_id=1, source_target_pairs={{0,12},{4,0},{8,4},{12,8},{1,13},{5,1},{9,5},{13,9},{2,14},{6,2},{... | collective-permute-start | bytes 3145736 | tf_op jit(solution)/shard_map/ppermute | solution.py:79
  14.1 11.4 %copy-start.13 = (bf16[256,2048]{1,0:T(8,128)(2,1)S(1)}, bf16[256,2048]{1,0:T(8,128)(2,1)}, u32[]{:S(2)}) copy-start(bf16[256,2048]{1,0:T(8,128)(2,1)} %param.5) | copy-start | bytes 3145732
  21.2 24.1 %collective-permute-start.4 = (bf16[2,128,1664]{2,1,0:T(8,128)(2,1)S(1)}, bf16[2,128,1664]{2,1,0:T(8,128)(2,1)S(1)}, u32[]{:S(2)}, u32[]{:S(2)}) collective-permute-start(bf16[2,128,1664]{2,1,0:T(8,128)(2,1)S(1)} %pad_maximum_fusion.3), channel_id=1, source_target_pairs={{0,2},{1,3},{2,0},{3,1},{4,6},{5,7},{6,4},{7,5},{8,10},{9,11},{10,... | collective-permute-start | bytes 2555912 | tf_op jit(solution)/shard_map/ppermute | solution.py:82
  24.0 22.0 %slice-start = ((s8[6815744]{0:T(1024)(128)(4,1)}), s8[4194304]{0:T(1024)(128)(4,1)S(1)}, s32[]{:S(2)}) async-start(s8[6815744]{0:T(1024)(128)(4,1)} %bitcast.113), calls=%async_computation.1 | async-start | bytes 8388608
  25.5 20.5 %slice-start.1 = ((s8[6815744]{0:T(1024)(128)(4,1)}), s8[2621440]{0:T(1024)(128)(4,1)S(1)}, s32[]{:S(2)}) async-start(s8[6815744]{0:T(1024)(128)(4,1)} %bitcast.113), calls=%async_computation.2 | async-start | bytes 5242880
  30.7 17.5 %copy-start.3 = (bf16[256,1664]{1,0:T(8,128)(2,1)}, bf16[256,1664]{1,0:T(8,128)(2,1)S(1)}, u32[]{:S(2)}) copy-start(bf16[256,1664]{1,0:T(8,128)(2,1)S(1)} %convolution_convert_fusion.2) | copy-start | bytes 2555908
  41.8 6.5 %copy-start.11 = (bf16[256,2048]{1,0:T(8,128)(2,1)}, bf16[256,2048]{1,0:T(8,128)(2,1)S(1)}, u32[]{:S(2)}) copy-start(bf16[256,2048]{1,0:T(8,128)(2,1)S(1)} %collective-permute-done.1) | copy-start | bytes 3145732
  41.9 21.8 %collective-permute-start.6 = (bf16[128,2048]{1,0:T(8,128)(2,1)S(1)}, bf16[128,2048]{1,0:T(8,128)(2,1)S(1)}, u32[]{:S(2)}, u32[]{:S(2)}) collective-permute-start(bf16[128,2048]{1,0:T(8,128)(2,1)S(1)} %slice.164), channel_id=1, source_target_pairs={{0,4},{4,8},{8,12},{12,0},{1,5},{5,9},{9,13},{13,1},{2,6},{6,10},{... | collective-permute-start | bytes 1572872 | tf_op jit(solution)/shard_map/ppermute | solution.py:99
  42.0 21.7 %collective-permute-start.7 = (bf16[128,2048]{1,0:T(8,128)(2,1)S(1)}, bf16[128,2048]{1,0:T(8,128)(2,1)S(1)}, u32[]{:S(2)}, u32[]{:S(2)}) collective-permute-start(bf16[128,2048]{1,0:T(8,128)(2,1)S(1)} %slice.165), channel_id=1, source_target_pairs={{0,12},{4,0},{8,4},{12,8},{1,13},{5,1},{9,5},{13,9},{2,14},{6,2},{... | collective-permute-start | bytes 1572872 | tf_op jit(solution)/shard_map/ppermute | solution.py:100
  45.7 4.9 %collective-permute-start.5 = (bf16[2,256,1664]{2,1,0:T(8,128)(2,1)S(1)}, bf16[2,256,1664]{2,1,0:T(8,128)(2,1)S(1)}, u32[]{:S(2)}, u32[]{:S(2)}) collective-permute-start(bf16[2,256,1664]{2,1,0:T(8,128)(2,1)S(1)} %bitcast.123), channel_id=1, source_target_pairs={{0,1},{1,0},{2,3},{3,2},{4,5},{5,4},{6,7},{7,6},{8,9},{9,8},{10,11... | collective-permute-start | bytes 5111816 | tf_op jit(solution)/shard_map/ppermute | solution.py:91
  48.2 2.3 %copy-start.5 = (bf16[256,1664]{1,0:T(8,128)(2,1)}, bf16[256,1664]{1,0:T(8,128)(2,1)S(1)}, u32[]{:S(2)}) copy-start(bf16[256,1664]{1,0:T(8,128)(2,1)S(1)} %convolution_convert_fusion.3) | copy-start | bytes 2555908
  50.5 15.3 %copy-start.7 = (bf16[256,1664]{1,0:T(8,128)(2,1)}, bf16[256,1664]{1,0:T(8,128)(2,1)S(1)}, u32[]{:S(2)}) copy-start(bf16[256,1664]{1,0:T(8,128)(2,1)S(1)} %convolution_convert_fusion.1) | copy-start | bytes 2555908
  61.7 2.0 %copy-start = (bf16[4,256,2048]{2,1,0:T(8,128)(2,1)}, bf16[4,256,2048]{2,1,0:T(8,128)(2,1)S(1)}, u32[]{:S(2)}) copy-start(bf16[4,256,2048]{2,1,0:T(8,128)(2,1)S(1)} %shard_map.58) | copy-start | bytes 12582916
  65.8 2.0 %copy-start.9 = (bf16[256,1664]{1,0:T(8,128)(2,1)}, bf16[256,1664]{1,0:T(8,128)(2,1)S(1)}, u32[]{:S(2)}) copy-start(bf16[256,1664]{1,0:T(8,128)(2,1)S(1)} %convolution_convert_fusion) | copy-start | bytes 2555908
  65.9 2.1 %copy-start.12 = (bf16[256,2048]{1,0:T(8,128)(2,1)S(1)}, bf16[256,2048]{1,0:T(8,128)(2,1)}, u32[]{:S(2)}) copy-start(bf16[256,2048]{1,0:T(8,128)(2,1)} %copy-done.11) | copy-start | bytes 3145732
  67.3 32.5 %collective-permute-start.10 = (bf16[2,256,1664]{2,1,0:T(8,128)(2,1)}, bf16[2,256,1664]{2,1,0:T(8,128)(2,1)}, u32[]{:S(2)}, u32[]{:S(2)}) collective-permute-start(bf16[2,256,1664]{2,1,0:T(8,128)(2,1)} %pad_maximum_fusion.1), channel_id=1, source_target_pairs={{0,1},{1,0},{2,3},{3,2},{4,5},{5,4},{6,7},{7,6},{8,9},{9,8},{10,11... | collective-permute-start | bytes 5111816 | tf_op jit(solution)/shard_map/ppermute | solution.py:109
  68.0 4.8 %copy-start.14 = (bf16[1024,2048]{1,0:T(8,128)(2,1)}, bf16[1024,2048]{1,0:T(8,128)(2,1)S(1)}, u32[]{:S(2)}) copy-start(bf16[1024,2048]{1,0:T(8,128)(2,1)S(1)} %constant_dynamic-update-slice_fusion) | copy-start | bytes 12582916
  72.9 1.7 copy-start.1
  75.6 18.4 %collective-permute-start.8 = (bf16[208,1024]{1,0:T(8,128)(2,1)}, bf16[208,1024]{1,0:T(8,128)(2,1)}, u32[]{:S(2)}, u32[]{:S(2)}) collective-permute-start(bf16[208,1024]{1,0:T(8,128)(2,1)} %get-tuple-element.68), channel_id=1, source_target_pairs={{0,32},{16,48},{32,64},{48,80},{64,96},{80,112},{96,0},{112,16},{1... | collective-permute-start | bytes 1277960 | tf_op jit(solution)/shard_map/ppermute | solution.py:124
  77.1 95.3 %all-to-all-start = ((bf16[4,256,2048]{2,1,0:T(8,128)(2,1)}), bf16[4,256,2048]{2,1,0:T(8,128)(2,1)}, u32[]{:S(2)}, u32[]{:S(2)}) async-start(bf16[4,256,2048]{2,1,0:T(8,128)(2,1)} %copy-done), calls=%async_computation | async-start | bytes 8388608 | tf_op jit(solution)/shard_map/all_to_all | solution.py:104
  82.0 11.8 %copy-start.2 = (bf16[1664,1024]{1,0:T(8,128)(2,1)S(1)}, bf16[1664,1024]{1,0:T(8,128)(2,1)}, u32[]{:S(2)}) copy-start(bf16[1664,1024]{1,0:T(8,128)(2,1)} %copy-done.1) | copy-start | bytes 10223620
  82.0 13.2 %collective-permute-start.9 = (bf16[208,1024]{1,0:T(8,128)(2,1)}, bf16[208,1024]{1,0:T(8,128)(2,1)S(1)}, u32[]{:S(2)}, u32[]{:S(2)}) collective-permute-start(bf16[208,1024]{1,0:T(8,128)(2,1)} %get-tuple-element.67), channel_id=1, source_target_pairs={{0,96},{16,112},{32,0},{48,16},{64,32},{80,48},{96,64},{112,80},{1... | collective-permute-start | bytes 1277960 | tf_op jit(solution)/shard_map/ppermute | solution.py:125
  90.4 9.4 %copy-start.4 = (bf16[256,1664]{1,0:T(8,128)(2,1)S(1)}, bf16[256,1664]{1,0:T(8,128)(2,1)}, u32[]{:S(2)}) copy-start(bf16[256,1664]{1,0:T(8,128)(2,1)} %copy-done.3) | copy-start | bytes 2555908
  90.4 9.4 %copy-start.6 = (bf16[256,1664]{1,0:T(8,128)(2,1)S(1)}, bf16[256,1664]{1,0:T(8,128)(2,1)}, u32[]{:S(2)}) copy-start(bf16[256,1664]{1,0:T(8,128)(2,1)} %copy-done.5) | copy-start | bytes 2555908
  90.5 9.4 %copy-start.8 = (bf16[256,1664]{1,0:T(8,128)(2,1)S(1)}, bf16[256,1664]{1,0:T(8,128)(2,1)}, u32[]{:S(2)}) copy-start(bf16[256,1664]{1,0:T(8,128)(2,1)} %copy-done.7) | copy-start | bytes 2555908
  90.5 9.4 %copy-start.10 = (bf16[256,1664]{1,0:T(8,128)(2,1)S(1)}, bf16[256,1664]{1,0:T(8,128)(2,1)}, u32[]{:S(2)}) copy-start(bf16[256,1664]{1,0:T(8,128)(2,1)} %copy-done.9) | copy-start | bytes 2555908
  90.5 14.5 %collective-permute-start.11 = (bf16[208,1024]{1,0:T(8,128)(2,1)S(1)}, bf16[208,1024]{1,0:T(8,128)(2,1)S(1)}, u32[]{:S(2)}, u32[]{:S(2)}) collective-permute-start(bf16[208,1024]{1,0:T(8,128)(2,1)S(1)} %get-tuple-element.60), channel_id=1, source_target_pairs={{0,32},{16,48},{32,64},{48,80},{64,96},{80,112},{96,0},{112,16},{1... | collective-permute-start | bytes 1277960 | tf_op jit(solution)/shard_map/ppermute | solution.py:124
  91.2 13.8 %collective-permute-start.12 = (bf16[208,1024]{1,0:T(8,128)(2,1)S(1)}, bf16[208,1024]{1,0:T(8,128)(2,1)S(1)}, u32[]{:S(2)}, u32[]{:S(2)}) collective-permute-start(bf16[208,1024]{1,0:T(8,128)(2,1)S(1)} %get-tuple-element.59), channel_id=1, source_target_pairs={{0,96},{16,112},{32,0},{48,16},{64,32},{80,48},{96,64},{112,80},{1... | collective-permute-start | bytes 1277960 | tf_op jit(solution)/shard_map/ppermute | solution.py:125
  96.5 25.1 %collective-permute-start.13 = (bf16[416,1024]{1,0:T(8,128)(2,1)S(1)}, bf16[416,1024]{1,0:T(8,128)(2,1)S(1)}, u32[]{:S(2)}, u32[]{:S(2)}) collective-permute-start(bf16[416,1024]{1,0:T(8,128)(2,1)S(1)} %get-tuple-element.45), channel_id=1, source_target_pairs={{0,32},{16,48},{32,64},{48,80},{64,96},{80,112},{96,0},{112,16},{1... | collective-permute-start | bytes 2555912 | tf_op jit(solution)/shard_map/ppermute | solution.py:133
  98.2 24.4 %collective-permute-start.14 = (bf16[416,1024]{1,0:T(8,128)(2,1)S(1)}, bf16[416,1024]{1,0:T(8,128)(2,1)S(1)}, u32[]{:S(2)}, u32[]{:S(2)}) collective-permute-start(bf16[416,1024]{1,0:T(8,128)(2,1)S(1)} %get-tuple-element.40), channel_id=1, source_target_pairs={{0,96},{16,112},{32,0},{48,16},{64,32},{80,48},{96,64},{112,80},{1... | collective-permute-start | bytes 2555912 | tf_op jit(solution)/shard_map/ppermute | solution.py:133
  102.1 25.1 %collective-permute-start.15 = (bf16[2,128,1664]{2,1,0:T(8,128)(2,1)S(1)}, bf16[2,128,1664]{2,1,0:T(8,128)(2,1)S(1)}, u32[]{:S(2)}, u32[]{:S(2)}) collective-permute-start(bf16[2,128,1664]{2,1,0:T(8,128)(2,1)S(1)} %pad_maximum_fusion.6), channel_id=1, source_target_pairs={{0,2},{1,3},{2,0},{3,1},{4,6},{5,7},{6,4},{7,5},{8,10},{9,11},{10,... | collective-permute-start | bytes 2555912 | tf_op jit(solution)/shard_map/ppermute | solution.py:144
  105.4 37.9 %collective-permute-start.17 = (bf16[416,1024]{1,0:T(8,128)(2,1)S(1)}, bf16[416,1024]{1,0:T(8,128)(2,1)S(1)}, u32[]{:S(2)}, u32[]{:S(2)}) collective-permute-start(bf16[416,1024]{1,0:T(8,128)(2,1)S(1)} %get-tuple-element.44), channel_id=1, source_target_pairs={{0,96},{16,112},{32,0},{48,16},{64,32},{80,48},{96,64},{112,80},{1... | collective-permute-start | bytes 2555912 | tf_op jit(solution)/shard_map/ppermute | solution.py:133
  122.6 20.7 %collective-permute-start.16 = (bf16[416,1024]{1,0:T(8,128)(2,1)S(1)}, bf16[416,1024]{1,0:T(8,128)(2,1)S(1)}, u32[]{:S(2)}, u32[]{:S(2)}) collective-permute-start(bf16[416,1024]{1,0:T(8,128)(2,1)S(1)} %get-tuple-element.49), channel_id=1, source_target_pairs={{0,32},{16,48},{32,64},{48,80},{64,96},{80,112},{96,0},{112,16},{1... | collective-permute-start | bytes 2555912 | tf_op jit(solution)/shard_map/ppermute | solution.py:133
  124.7 28.0 %collective-permute-start.20 = (bf16[208,1024]{1,0:T(8,128)(2,1)S(1)}, bf16[208,1024]{1,0:T(8,128)(2,1)S(1)}, u32[]{:S(2)}, u32[]{:S(2)}) collective-permute-start(bf16[208,1024]{1,0:T(8,128)(2,1)S(1)} %select_convert_fusion.1), channel_id=1, source_target_pairs={{0,16},{16,0},{32,48},{48,32},{64,80},{80,64},{96,112},{112,96},{1... | collective-permute-start | bytes 1277960 | tf_op jit(solution)/shard_map/ppermute | solution.py:152
  127.4 32.7 %collective-permute-start.19 = (bf16[128,1664]{1,0:T(8,128)(2,1)S(1)}, bf16[128,1664]{1,0:T(8,128)(2,1)S(1)}, u32[]{:S(2)}, u32[]{:S(2)}) collective-permute-start(bf16[128,1664]{1,0:T(8,128)(2,1)S(1)} %get-tuple-element.54), channel_id=1, source_target_pairs={{2,0},{5,1},{8,2},{15,3},{3,4},{6,5},{9,6},{12,7},{0,8},{7,9},{10,... | collective-permute-start | bytes 1277960 | tf_op jit(solution)/shard_map/ppermute | solution.py:160
  143.3 16.8 %collective-permute-start.18 = (bf16[128,1664]{1,0:T(8,128)(2,1)S(1)}, bf16[128,1664]{1,0:T(8,128)(2,1)S(1)}, u32[]{:S(2)}, u32[]{:S(2)}) collective-permute-start(bf16[128,1664]{1,0:T(8,128)(2,1)S(1)} %get-tuple-element.53), channel_id=1, source_target_pairs={{0,0},{7,1},{10,2},{13,3},{1,4},{4,5},{11,6},{14,7},{2,8},{5,9},{8... | collective-permute-start | bytes 1277960 | tf_op jit(solution)/shard_map/ppermute | solution.py:159
  150.4 20.5 %collective-permute-start.21 = (bf16[208,1024]{1,0:T(8,128)(2,1)S(1)}, bf16[208,1024]{1,0:T(8,128)(2,1)S(1)}, u32[]{:S(2)}, u32[]{:S(2)}) collective-permute-start(bf16[208,1024]{1,0:T(8,128)(2,1)S(1)} %select_convert_fusion), channel_id=1, source_target_pairs={{0,16},{16,0},{32,48},{48,32},{64,80},{80,64},{96,112},{112,96},{1... | collective-permute-start | bytes 1277960 | tf_op jit(solution)/shard_map/ppermute | solution.py:152

commit v3 on v2

--- a/solution.py
+++ b/solution.py
@@ -38,7 +38,7 @@
 COST = pl.CostEstimate(flops=1000, bytes_accessed=1000, transcendentals=0)
 
 
-def tokens_by_width(place, hs, w, block=256):
+def tokens_by_width(place, hs, w, block=512):
     def kernel(place_ref, *refs):
         w_ref, o_ref = refs[-2:]
         o = dot(jnp.concatenate([r[...] for r in refs[:-2]], axis=0), w_ref[...], 1, 0).astype(BF)
@@ -58,7 +58,7 @@
         ),
         out_shape=jax.ShapeDtypeStruct((4, rows, n), BF),
         cost_estimate=COST,
-        compiler_params=params(16),
+        compiler_params=params(24),
     )(place, *hs, w)
 
 
@@ -159,11 +159,11 @@
     h_a = lax.ppermute(g_a, ("row", "col"), FROM_PLANE)
     h_b = lax.ppermute(g_b, ("row", "col"), FROM_PLANE_X)
 
-    v1, v3 = after(g_b, v1, v3)
+    (o_in,) = after(g_b, o_in)
+    output = jnp.sum(o_in.astype(F32), axis=0).astype(BF)
+
+    v1, v3 = after(output, v1, v3)
     x_out, mine1, x1 = over_x(1, v1, v3)
-
-    (o_in,) = after(x_out, o_in)
-    output = jnp.sum(o_in.astype(F32), axis=0).astype(BF)
 
     weight_grad = jnp.concatenate([mine0 + x0.astype(F32), mine1 + x1.astype(F32)], axis=1)
     hidden_grad = jnp.concatenate([h_a, h_b], axis=0)

time: 177 us -> 167 us (0.944)
  waiting for transfers between devices: 61.8 us -> 47.2 us
  other arithmetic: 14.8 us -> 20.7 us
  starting transfers between devices: 56.8 us -> 54.1 us
    ppermute x1, waiting for transfers between devices: 0.01 us -> 13.8 us  [shards(): h_b = lax.ppermute(g_b, ('row', 'col'), FROM_PLANE_X)]
    ppermute x2, waiting for transfers between devices: 24.5 us -> 13 us  [second(): lax.ppermute(w1, 'dp', Y_UP)]
    ppermute x2, waiting for transfers between devices: 9.9 us -> 0.13 us  [over_x(): return (out, jnp.where(low, t[:hf], t[hf:]), lax.ppermute(out, 'dp', XHI))]
    ppermute x1, waiting for transfers between devices: 7.21 us -> 0.01 us  [shards(): h_a = lax.ppermute(g_a, ('row', 'col'), FROM_PLANE)]
    ppermute x1, starting transfers between devices: 4.91 us -> 2.43 us  [shards(): h_b = lax.ppermute(g_b, ('row', 'col'), FROM_PLANE_X)]
    unnamed x38 -> x40, local copies, waits for them, and re-layouts: 5.37 us -> 5.38 us
  transfers between devices with their start and end apart: 23 -> 23, of which waited for: 8 -> 8; matrix products, arithmetic and copies ran while one was open for 19% -> 26% of each run, Pallas kernels for 6% -> 6%
where the time goes in v3:
time: 167 us; the launch traced here: 165 us
  starting transfers between devices  54.1 us (32%)
  waiting for transfers between devices  47.2 us (28%)
  matrix products  22.7 us (14%)
  other arithmetic  20.7 us (12%)
  local copies, waits for them, and re-layouts  9.99 us (6%)
  Pallas kernels  9.14 us (5%)
    dot_general x6, matrix products, dot(): lax.dot_general(a, b, (((ca,), (cb,)), ((), ())), preferred_element_type=...  22.7 us
    ppermute x1, waiting for transfers between devices, shards(): h_b = lax.ppermute(g_b, ('row', 'col'), FROM_PLANE_X)  13.8 us
    ppermute x2, waiting for transfers between devices, second(): lax.ppermute(w1, 'dp', Y_UP)  13 us
    ppermute x1, waiting for transfers between devices, shards(): u3 = lax.ppermute(upstream, 'row', Z_UP)  11.1 us
    pallas_call x1, Pallas kernels, tokens_by_width(): pl.pallas_call(kernel, grid_spec=pltpu.PrefetchScalarGridSpec(num_scalar_...  9.14 us
    ppermute x1, starting transfers between devices, shards(): h_a = lax.ppermute(g_a, ('row', 'col'), FROM_PLANE)  7.44 us
    ppermute x1, waiting for transfers between devices, shards(): own_a = lax.ppermute(hidden[:half], ('row', 'col'), TO_PLANE)  7 us
    ppermute x1, starting transfers between devices, shards(): own_a = lax.ppermute(hidden[:half], ('row', 'col'), TO_PLANE)  5.77 us
  transfers between devices with their start and end apart: 23, of which 8 were waited for; matrix products, arithmetic and copies ran while one was open for 26% of the time, Pallas kernels for 6%

profile of v3, /device:TPU:2, one launch (start us, length us, event | category | flops | bytes accessed | tf_op | source)
XLA Modules:
  0.0 165.1 jit_solution(2174596184203127731)
XLA Ops:
  0.6 2.0 %fusion.36 = (bf16[128,1664]{1,0:T(8,128)(2,1)}, bf16[128,1664]{1,0:T(8,128)(2,1)S(1)}) fusion(bf16[256,1664]{1,0:T(8,128)(2,1)} %param.3), kind=kLoop, calls=%fused_computation.97 | loop fusion | bytes 1703936 | tf_op jit(solution)/shard_map/slice | solution.py:76
  2.6 5.8 %collective-permute-start = (bf16[128,1664]{1,0:T(8,128)(2,1)}, bf16[128,1664]{1,0:T(8,128)(2,1)S(1)}, u32[]{:S(2)}, u32[]{:S(2)}) collective-permute-start(bf16[128,1664]{1,0:T(8,128)(2,1)} %get-tuple-element.83), channel_id=1, source_target_pairs={{0,0},{1,7},{2,10},{3,13},{4,1},{5,4},{6,11},{7,14},{8,2},{9,5},{1... | collective-permute-start | bytes 1277960 | tf_op jit(solution)/shard_map/ppermute | solution.py:76
  8.4 2.5 %collective-permute-start.1 = (bf16[128,1664]{1,0:T(8,128)(2,1)S(1)}, bf16[128,1664]{1,0:T(8,128)(2,1)S(1)}, u32[]{:S(2)}, u32[]{:S(2)}) collective-permute-start(bf16[128,1664]{1,0:T(8,128)(2,1)S(1)} %get-tuple-element.84), channel_id=1, source_target_pairs={{0,2},{1,5},{2,8},{3,15},{4,3},{5,6},{6,9},{7,12},{8,0},{9,7},{10,... | collective-permute-start | bytes 1277960 | tf_op jit(solution)/shard_map/ppermute | solution.py:77
  10.9 3.2 %collective-permute-start.6 = (bf16[256,2048]{1,0:T(8,128)(2,1)}, bf16[256,2048]{1,0:T(8,128)(2,1)S(1)}, u32[]{:S(2)}, u32[]{:S(2)}) collective-permute-start(bf16[256,2048]{1,0:T(8,128)(2,1)} %param.5), channel_id=1, source_target_pairs={{0,12},{4,0},{8,4},{12,8},{1,13},{5,1},{9,5},{13,9},{2,14},{6,2},{... | collective-permute-start | bytes 3145736 | tf_op jit(solution)/shard_map/ppermute | solution.py:79
  14.1 7.0 %collective-permute-done = bf16[128,1664]{1,0:T(8,128)(2,1)S(1)} collective-permute-done((bf16[128,1664]{1,0:T(8,128)(2,1)}, bf16[128,1664]{1,0:T(8,128)(2,1)S(1)}, u32[]{:S(2)}, u32[]{:S(2)}) %collective-permute-start) | collective-permute-done | bytes 426016 | tf_op jit(solution)/shard_map/ppermute | solution.py:76
  21.2 2.8 %collective-permute-start.2 = (bf16[2,128,1664]{2,1,0:T(8,128)(2,1)S(1)}, bf16[2,128,1664]{2,1,0:T(8,128)(2,1)S(1)}, u32[]{:S(2)}, u32[]{:S(2)}) collective-permute-start(bf16[2,128,1664]{2,1,0:T(8,128)(2,1)S(1)} %pad_maximum_fusion.3), channel_id=1, source_target_pairs={{0,2},{1,3},{2,0},{3,1},{4,6},{5,7},{6,4},{7,5},{8,10},{9,11},{10,... | collective-permute-start | bytes 2555912 | tf_op jit(solution)/shard_map/ppermute | solution.py:82
  24.0 1.5 constant_dynamic-update-slice_fusion.4
  25.6 5.2 %convolution_convert_fusion = bf16[256,1664]{1,0:T(8,128)(2,1)S(1)} fusion(bf16[256,2048]{1,0:T(8,128)(2,1)S(1)} %copy-done.14, bf16[1664,2048]{1,0:T(8,128)(2,1)} %refs_4_.1), kind=kOutput, calls=%fused_computation.16 | convolution fusion | flops 1745256448 | bytes 8716288 | tf_op jit(solution)/shard_map/dot_general | solution.py:27
  30.8 11.1 %collective-permute-done.4 = bf16[256,2048]{1,0:T(8,128)(2,1)S(1)} collective-permute-done((bf16[256,2048]{1,0:T(8,128)(2,1)}, bf16[256,2048]{1,0:T(8,128)(2,1)S(1)}, u32[]{:S(2)}, u32[]{:S(2)}) %collective-permute-start.4) | collective-permute-done | bytes 1048608 | tf_op jit(solution)/shard_map/ppermute | solution.py:78
  42.0 3.3 %collective-permute-start.7 = (bf16[128,2048]{1,0:T(8,128)(2,1)S(1)}, bf16[128,2048]{1,0:T(8,128)(2,1)S(1)}, u32[]{:S(2)}, u32[]{:S(2)}) collective-permute-start(bf16[128,2048]{1,0:T(8,128)(2,1)S(1)} %slice.165), channel_id=1, source_target_pairs={{0,12},{4,0},{8,4},{12,8},{1,13},{5,1},{9,5},{13,9},{2,14},{6,2},{... | collective-permute-start | bytes 1572872 | tf_op jit(solution)/shard_map/ppermute | solution.py:100
  45.3 0.2 select_bitcast_fusion.3
  45.5 0.3 pad_maximum_fusion
  45.7 0.3 collective-permute-start.3
  46.0 2.1 %convolution_convert_fusion.1 = bf16[256,1664]{1,0:T(8,128)(2,1)S(1)} fusion(bf16[256,2048]{1,0:T(8,128)(2,1)S(1)} %collective-permute-done.6, bf16[1664,2048]{1,0:T(8,128)(2,1)S(1)} %bitcast.114), kind=kOutput, calls=%fused_computation.17 | convolution fusion | flops 1745256448 | bytes 8716288 | tf_op jit(solution)/shard_map/dot_general | solution.py:27
  48.3 0.1 select_bitcast_fusion.1
  48.4 2.1 %convolution_convert_fusion.2 = bf16[256,1664]{1,0:T(8,128)(2,1)S(1)} fusion(bf16[256,2048]{1,0:T(8,128)(2,1)S(1)} %collective-permute-done.4, bf16[1664,2048]{1,0:T(8,128)(2,1)S(1)} %bitcast.114), kind=kOutput, calls=%fused_computation.18 | convolution fusion | flops 1745256448 | bytes 8716288 | tf_op jit(solution)/shard_map/dot_general | solution.py:27
  50.5 0.2 pad_maximum_fusion.4
  50.7 0.5 bitcast_select_fusion
  51.2 9.1 %shard_map.58 = bf16[4,256,2048]{2,1,0:T(8,128)(2,1)S(1)} custom-call(s32[1]{0:T(128)} %bitcast.place_ref, bf16[256,1664]{1,0:T(8,128)(2,1)S(1)} %get-tuple-element.34.refs_0_, bf16[256,1664]{1,0:T(8,128)(2,1)S(1)} %get-tuple-element.35.refs_1_, bf16[256,1664]{1,0:T(8,128)(2,1)S(1)} %get-tuple-element.36.refs_2_, ...), custom_call_target="tpu_custom_call" | custom-call | flops 1000 | bytes 1000 | tf_op jit(solution)/shard_map/pallas_call | solution.py:50
  60.3 2.0 %copy-done = bf16[4,256,2048]{2,1,0:T(8,128)(2,1)} copy-done((bf16[4,256,2048]{2,1,0:T(8,128)(2,1)}, bf16[4,256,2048]{2,1,0:T(8,128)(2,1)S(1)}, u32[]{:S(2)}) %copy-start) | copy-done | bytes 4194328
  62.3 2.1 %convolution_convert_fusion.3 = bf16[256,1664]{1,0:T(8,128)(2,1)S(1)} fusion(bf16[1664,2048]{1,0:T(8,128)(2,1)S(1)} %bitcast.114, bf16[128,2048]{1,0:T(8,128)(2,1)S(1)} %collective-permute-done.7, bf16[128,2048]{1,0:T(8,128)(2,1)S(1)} %collective-permute-done.5), kind=kOutput, calls=%fused_computation.19 | convolution fusion | flops 1747353600 | bytes 8716288 | tf_op jit(solution)/shard_map/dot_general | solution.py:27
  64.5 0.1 select_bitcast_fusion
  64.6 1.4 pad_maximum_fusion.1
  65.9 0.5 collective-permute-start.10
  66.5 0.1 constant_dynamic-update-slice_fusion
  66.6 4.8 %multiply_convert_fusion.1 = bf16[1664,1024]{1,0:T(8,128)(2,1)S(1)} fusion(bf16[256,1664]{1,0:T(8,128)(2,1)S(1)} %get-tuple-element.37.refs_3_, bf16[256,1664]{1,0:T(8,128)(2,1)S(1)} %get-tuple-element.36.refs_2_, bf16[256,1664]{1,0:T(8,128)(2,1)S(1)} %get-tuple-element.35.refs_1_, bf16[256,1664]{1,0:T(8,128)(2,1)S(1)} %get-tuple-element.34.refs_0_, ...), kind=kOutput, calls=%fused_computation.1 | convolution fusion | flops 3506700288 | bytes 8912896 | tf_op jit(solution)/shard_map/dot_general | solution.py:27
  71.5 1.7 %copy-done.2 = bf16[1664,1024]{1,0:T(8,128)(2,1)} copy-done((bf16[1664,1024]{1,0:T(8,128)(2,1)}, bf16[1664,1024]{1,0:T(8,128)(2,1)S(1)}, u32[]{:S(2)}) %copy-start.2) | copy-done | bytes 3407896
  73.2 1.0 dynamic-slice_bitcast_fusion.8
  74.2 1.6 collective-permute-start.8
  75.8 4.9 %all-to-all-start = ((bf16[4,256,2048]{2,1,0:T(8,128)(2,1)}), bf16[4,256,2048]{2,1,0:T(8,128)(2,1)}, u32[]{:S(2)}, u32[]{:S(2)}) async-start(bf16[4,256,2048]{2,1,0:T(8,128)(2,1)} %copy-done), calls=%async_computation | async-start | bytes 8388608 | tf_op jit(solution)/shard_map/all_to_all | solution.py:104
  80.6 1.9 %collective-permute-start.9 = (bf16[208,1024]{1,0:T(8,128)(2,1)}, bf16[208,1024]{1,0:T(8,128)(2,1)S(1)}, u32[]{:S(2)}, u32[]{:S(2)}) collective-permute-start(bf16[208,1024]{1,0:T(8,128)(2,1)} %get-tuple-element.67), channel_id=1, source_target_pairs={{0,96},{16,112},{32,0},{48,16},{64,32},{80,48},{96,64},{112,80},{1... | collective-permute-start | bytes 1277960 | tf_op jit(solution)/shard_map/ppermute | solution.py:125
  82.6 6.4 %multiply_convert_fusion = bf16[1664,1024]{1,0:T(8,128)(2,1)S(1)} fusion(bf16[256,1664]{1,0:T(8,128)(2,1)S(1)} %get-tuple-element.37.refs_3_, bf16[256,1664]{1,0:T(8,128)(2,1)S(1)} %get-tuple-element.36.refs_2_, bf16[256,1664]{1,0:T(8,128)(2,1)S(1)} %get-tuple-element.35.refs_1_, bf16[256,1664]{1,0:T(8,128)(2,1)S(1)} %get-tuple-element.34.refs_0_, ...), kind=kOutput, calls=%fused_computation | convolution fusion | flops 3506700288 | bytes 8912896 | tf_op jit(solution)/shard_map/dot_general | solution.py:27
  89.1 0.7 collective-permute-start.11
  89.8 2.6 %collective-permute-start.12 = (bf16[208,1024]{1,0:T(8,128)(2,1)S(1)}, bf16[208,1024]{1,0:T(8,128)(2,1)S(1)}, u32[]{:S(2)}, u32[]{:S(2)}) collective-permute-start(bf16[208,1024]{1,0:T(8,128)(2,1)S(1)} %get-tuple-element.59), channel_id=1, source_target_pairs={{0,96},{16,112},{32,0},{48,16},{64,32},{80,48},{96,64},{112,80},{1... | collective-permute-start | bytes 1277960 | tf_op jit(solution)/shard_map/ppermute | solution.py:125
  92.4 0.1 dynamic-slice_bitcast_fusion.2
  92.6 1.2 collective-permute-done.9
  93.8 1.3 fusion.30
  95.1 1.6 collective-permute-start.13
  96.8 1.7 %collective-permute-start.14 = (bf16[416,1024]{1,0:T(8,128)(2,1)S(1)}, bf16[416,1024]{1,0:T(8,128)(2,1)S(1)}, u32[]{:S(2)}, u32[]{:S(2)}) collective-permute-start(bf16[416,1024]{1,0:T(8,128)(2,1)S(1)} %get-tuple-element.40), channel_id=1, source_target_pairs={{0,96},{16,112},{32,0},{48,16},{64,32},{80,48},{96,64},{112,80},{1... | collective-permute-start | bytes 2555912 | tf_op jit(solution)/shard_map/ppermute | solution.py:133
  98.5 2.0 %convert_add_fusion.3 = (f32[256,1664]{1,0:T(8,128)S(1)}, f32[256,1664]{1,0:T(8,128)S(1)}) fusion(bf16[2,256,1664]{2,1,0:T(8,128)(2,1)} %collective-permute-done.10, bf16[256,1664]{1,0:T(8,128)(2,1)S(1)} %copy-done.11, bf16[256,1664]{1,0:T(8,128)(2,1)S(1)} %copy-done.9, pred[]{:T(512)S(6)} %eq.19, bf16[256,1664]{1,0:T(8,128)(2,1)S(1)} %copy-done.5, ...), kind=kLoop, calls=%fused_computation.30 | loop fusion | flops 3407872 | bytes 8519681 | tf_op jit(solution)/shard_map/add | solution.py:140
  100.4 0.2 fusion.27
  100.7 2.8 %collective-permute-start.15 = (bf16[2,128,1664]{2,1,0:T(8,128)(2,1)S(1)}, bf16[2,128,1664]{2,1,0:T(8,128)(2,1)S(1)}, u32[]{:S(2)}, u32[]{:S(2)}) collective-permute-start(bf16[2,128,1664]{2,1,0:T(8,128)(2,1)S(1)} %pad_maximum_fusion.6), channel_id=1, source_target_pairs={{0,2},{1,3},{2,0},{3,1},{4,6},{5,7},{6,4},{7,5},{8,10},{9,11},{10,... | collective-permute-start | bytes 2555912 | tf_op jit(solution)/shard_map/ppermute | solution.py:144
  103.5 1.3 dynamic-slice_bitcast_fusion
  104.8 1.2 fusion.32
  106.0 1.5 collective-permute-start.20
  107.6 12.7 %collective-permute-done.13 = bf16[416,1024]{1,0:T(8,128)(2,1)S(1)} collective-permute-done((bf16[416,1024]{1,0:T(8,128)(2,1)S(1)}, bf16[416,1024]{1,0:T(8,128)(2,1)S(1)}, u32[]{:S(2)}, u32[]{:S(2)}) %collective-permute-start.13) | collective-permute-done | bytes 852000 | tf_op jit(solution)/shard_map/ppermute | solution.py:133
  120.3 0.9 collective-permute-done.14
  121.2 1.6 collective-permute-start.19
  122.8 0.4 fusion.17
  123.2 0.8 select_convert_fusion.1
  124.0 2.4 %collective-permute-start.18 = (bf16[208,1024]{1,0:T(8,128)(2,1)}, bf16[208,1024]{1,0:T(8,128)(2,1)}, u32[]{:S(2)}, u32[]{:S(2)}) collective-permute-start(bf16[208,1024]{1,0:T(8,128)(2,1)} %select_convert_fusion.1), channel_id=1, source_target_pairs={{0,16},{16,0},{32,48},{48,32},{64,80},{80,64},{96,112},{112,96},{1... | collective-permute-start | bytes 1277960 | tf_op jit(solution)/shard_map/ppermute | solution.py:152
  126.4 1.2 fusion.21
  127.6 7.4 %collective-permute-start.16 = (bf16[128,1664]{1,0:T(8,128)(2,1)}, bf16[128,1664]{1,0:T(8,128)(2,1)}, u32[]{:S(2)}, u32[]{:S(2)}) collective-permute-start(bf16[128,1664]{1,0:T(8,128)(2,1)} %get-tuple-element.53), channel_id=1, source_target_pairs={{0,0},{7,1},{10,2},{13,3},{1,4},{4,5},{11,6},{14,7},{2,8},{5,9},{8... | collective-permute-start | bytes 1277960 | tf_op jit(solution)/shard_map/ppermute | solution.py:159
  135.1 2.4 %collective-permute-start.17 = (bf16[128,1664]{1,0:T(8,128)(2,1)}, bf16[128,1664]{1,0:T(8,128)(2,1)}, u32[]{:S(2)}, u32[]{:S(2)}) collective-permute-start(bf16[128,1664]{1,0:T(8,128)(2,1)} %get-tuple-element.54), channel_id=1, source_target_pairs={{2,0},{5,1},{8,2},{15,3},{3,4},{6,5},{9,6},{12,7},{0,8},{7,9},{10,... | collective-permute-start | bytes 1277960 | tf_op jit(solution)/shard_map/ppermute | solution.py:160
  137.5 4.3 %reduce_sum.12 = bf16[256,2048]{1,0:T(8,128)(2,1)} reduce(bf16[4,256,2048]{2,1,0:T(8,128)(2,1)} %all-to-all-done, bf16[]{:T(256)} %constant.99.clone.1), dimensions={0}, to_apply=%region_0.1 | reduce | flops 1572864 | bytes 5242882 | tf_op jit(solution)/shard_map/reduce_sum | solution.py:163
  141.8 0.3 collective-permute-done.19
  142.1 1.6 fusion.16
  143.8 2.5 %collective-permute-start.21 = (bf16[208,1024]{1,0:T(8,128)(2,1)S(1)}, bf16[208,1024]{1,0:T(8,128)(2,1)S(1)}, u32[]{:S(2)}, u32[]{:S(2)}) collective-permute-start(bf16[208,1024]{1,0:T(8,128)(2,1)S(1)} %select_convert_fusion), channel_id=1, source_target_pairs={{0,16},{16,0},{32,48},{48,32},{64,80},{80,64},{96,112},{112,96},{1... | collective-permute-start | bytes 1277960 | tf_op jit(solution)/shard_map/ppermute | solution.py:152
  146.3 1.2 convert_add_fusion.11
  147.5 13.8 %collective-permute-done.17 = bf16[128,1664]{1,0:T(8,128)(2,1)} collective-permute-done((bf16[128,1664]{1,0:T(8,128)(2,1)}, bf16[128,1664]{1,0:T(8,128)(2,1)}, u32[]{:S(2)}, u32[]{:S(2)}) %collective-permute-start.17) | collective-permute-done | bytes 426016 | tf_op jit(solution)/shard_map/ppermute | solution.py:160
  161.3 2.1 %pad_maximum_fusion.7 = bf16[256,1664]{1,0:T(8,128)(2,1)} fusion(bf16[128,1664]{1,0:T(8,128)(2,1)} %collective-permute-done.17, bf16[128,1664]{1,0:T(8,128)(2,1)} %collective-permute-done.16), kind=kLoop, calls=%fused_computation.40 | loop fusion | flops 1703936 | bytes 1703936 | tf_op jit(solution)/shard_map/concatenate | solution.py:169
  163.4 0.1 collective-permute-done.21
  163.5 0.2 convert_add_fusion.10
  163.8 1.3 pad_maximum_fusion.2
  (61 shorter events, 0.8 us)
Async XLA Ops:
  2.6 18.6 %collective-permute-start = (bf16[128,1664]{1,0:T(8,128)(2,1)}, bf16[128,1664]{1,0:T(8,128)(2,1)S(1)}, u32[]{:S(2)}, u32[]{:S(2)}) collective-permute-start(bf16[128,1664]{1,0:T(8,128)(2,1)} %get-tuple-element.83), channel_id=1, source_target_pairs={{0,0},{1,7},{2,10},{3,13},{4,1},{5,4},{6,11},{7,14},{8,2},{9,5},{1... | collective-permute-start | bytes 1277960 | tf_op jit(solution)/shard_map/ppermute | solution.py:76
  8.4 12.8 %collective-permute-start.1 = (bf16[128,1664]{1,0:T(8,128)(2,1)S(1)}, bf16[128,1664]{1,0:T(8,128)(2,1)S(1)}, u32[]{:S(2)}, u32[]{:S(2)}) collective-permute-start(bf16[128,1664]{1,0:T(8,128)(2,1)S(1)} %get-tuple-element.84), channel_id=1, source_target_pairs={{0,2},{1,5},{2,8},{3,15},{4,3},{5,6},{6,9},{7,12},{8,0},{9,7},{10,... | collective-permute-start | bytes 1277960 | tf_op jit(solution)/shard_map/ppermute | solution.py:77
  10.8 31.0 %collective-permute-start.4 = (bf16[256,2048]{1,0:T(8,128)(2,1)}, bf16[256,2048]{1,0:T(8,128)(2,1)S(1)}, u32[]{:S(2)}, u32[]{:S(2)}) collective-permute-start(bf16[256,2048]{1,0:T(8,128)(2,1)} %param.5), channel_id=1, source_target_pairs={{0,4},{4,8},{8,12},{12,0},{1,5},{5,9},{9,13},{13,1},{2,6},{6,10},{... | collective-permute-start | bytes 3145736 | tf_op jit(solution)/shard_map/ppermute | solution.py:78
  10.9 31.0 %collective-permute-start.6 = (bf16[256,2048]{1,0:T(8,128)(2,1)}, bf16[256,2048]{1,0:T(8,128)(2,1)S(1)}, u32[]{:S(2)}, u32[]{:S(2)}) collective-permute-start(bf16[256,2048]{1,0:T(8,128)(2,1)} %param.5), channel_id=1, source_target_pairs={{0,12},{4,0},{8,4},{12,8},{1,13},{5,1},{9,5},{13,9},{2,14},{6,2},{... | collective-permute-start | bytes 3145736 | tf_op jit(solution)/shard_map/ppermute | solution.py:79
  14.1 11.4 %copy-start.14 = (bf16[256,2048]{1,0:T(8,128)(2,1)S(1)}, bf16[256,2048]{1,0:T(8,128)(2,1)}, u32[]{:S(2)}) copy-start(bf16[256,2048]{1,0:T(8,128)(2,1)} %param.5) | copy-start | bytes 3145732
  21.2 24.1 %collective-permute-start.2 = (bf16[2,128,1664]{2,1,0:T(8,128)(2,1)S(1)}, bf16[2,128,1664]{2,1,0:T(8,128)(2,1)S(1)}, u32[]{:S(2)}, u32[]{:S(2)}) collective-permute-start(bf16[2,128,1664]{2,1,0:T(8,128)(2,1)S(1)} %pad_maximum_fusion.3), channel_id=1, source_target_pairs={{0,2},{1,3},{2,0},{3,1},{4,6},{5,7},{6,4},{7,5},{8,10},{9,11},{10,... | collective-permute-start | bytes 2555912 | tf_op jit(solution)/shard_map/ppermute | solution.py:82
  24.0 22.0 %slice-start = ((s8[6815744]{0:T(1024)(128)(4,1)}), s8[4194304]{0:T(1024)(128)(4,1)S(1)}, s32[]{:S(2)}) async-start(s8[6815744]{0:T(1024)(128)(4,1)} %bitcast.113), calls=%async_computation.1 | async-start | bytes 8388608
  25.5 20.5 %slice-start.1 = ((s8[6815744]{0:T(1024)(128)(4,1)}), s8[2621440]{0:T(1024)(128)(4,1)S(1)}, s32[]{:S(2)}) async-start(s8[6815744]{0:T(1024)(128)(4,1)} %bitcast.113), calls=%async_computation.2 | async-start | bytes 5242880
  30.7 17.5 %copy-start.4 = (bf16[256,1664]{1,0:T(8,128)(2,1)}, bf16[256,1664]{1,0:T(8,128)(2,1)S(1)}, u32[]{:S(2)}) copy-start(bf16[256,1664]{1,0:T(8,128)(2,1)S(1)} %convolution_convert_fusion) | copy-start | bytes 2555908
  41.8 6.5 %copy-start.12 = (bf16[256,2048]{1,0:T(8,128)(2,1)}, bf16[256,2048]{1,0:T(8,128)(2,1)S(1)}, u32[]{:S(2)}) copy-start(bf16[256,2048]{1,0:T(8,128)(2,1)S(1)} %collective-permute-done.4) | copy-start | bytes 3145732
  41.9 20.4 %collective-permute-start.5 = (bf16[128,2048]{1,0:T(8,128)(2,1)S(1)}, bf16[128,2048]{1,0:T(8,128)(2,1)S(1)}, u32[]{:S(2)}, u32[]{:S(2)}) collective-permute-start(bf16[128,2048]{1,0:T(8,128)(2,1)S(1)} %slice.164), channel_id=1, source_target_pairs={{0,4},{4,8},{8,12},{12,0},{1,5},{5,9},{9,13},{13,1},{2,6},{6,10},{... | collective-permute-start | bytes 1572872 | tf_op jit(solution)/shard_map/ppermute | solution.py:99
  42.0 20.3 %collective-permute-start.7 = (bf16[128,2048]{1,0:T(8,128)(2,1)S(1)}, bf16[128,2048]{1,0:T(8,128)(2,1)S(1)}, u32[]{:S(2)}, u32[]{:S(2)}) collective-permute-start(bf16[128,2048]{1,0:T(8,128)(2,1)S(1)} %slice.165), channel_id=1, source_target_pairs={{0,12},{4,0},{8,4},{12,8},{1,13},{5,1},{9,5},{13,9},{2,14},{6,2},{... | collective-permute-start | bytes 1572872 | tf_op jit(solution)/shard_map/ppermute | solution.py:100
  45.7 4.9 %collective-permute-start.3 = (bf16[2,256,1664]{2,1,0:T(8,128)(2,1)S(1)}, bf16[2,256,1664]{2,1,0:T(8,128)(2,1)S(1)}, u32[]{:S(2)}, u32[]{:S(2)}) collective-permute-start(bf16[2,256,1664]{2,1,0:T(8,128)(2,1)S(1)} %bitcast.123), channel_id=1, source_target_pairs={{0,1},{1,0},{2,3},{3,2},{4,5},{5,4},{6,7},{7,6},{8,9},{9,8},{10,11... | collective-permute-start | bytes 5111816 | tf_op jit(solution)/shard_map/ppermute | solution.py:91
  48.2 2.3 %copy-start.6 = (bf16[256,1664]{1,0:T(8,128)(2,1)}, bf16[256,1664]{1,0:T(8,128)(2,1)S(1)}, u32[]{:S(2)}) copy-start(bf16[256,1664]{1,0:T(8,128)(2,1)S(1)} %convolution_convert_fusion.1) | copy-start | bytes 2555908
  50.5 13.9 %copy-start.8 = (bf16[256,1664]{1,0:T(8,128)(2,1)}, bf16[256,1664]{1,0:T(8,128)(2,1)S(1)}, u32[]{:S(2)}) copy-start(bf16[256,1664]{1,0:T(8,128)(2,1)S(1)} %convolution_convert_fusion.2) | copy-start | bytes 2555908
  60.3 2.0 %copy-start = (bf16[4,256,2048]{2,1,0:T(8,128)(2,1)}, bf16[4,256,2048]{2,1,0:T(8,128)(2,1)S(1)}, u32[]{:S(2)}) copy-start(bf16[4,256,2048]{2,1,0:T(8,128)(2,1)S(1)} %shard_map.58) | copy-start | bytes 12582916
  64.4 2.0 %copy-start.10 = (bf16[256,1664]{1,0:T(8,128)(2,1)}, bf16[256,1664]{1,0:T(8,128)(2,1)S(1)}, u32[]{:S(2)}) copy-start(bf16[256,1664]{1,0:T(8,128)(2,1)S(1)} %convolution_convert_fusion.3) | copy-start | bytes 2555908
  64.5 2.1 %copy-start.13 = (bf16[256,2048]{1,0:T(8,128)(2,1)S(1)}, bf16[256,2048]{1,0:T(8,128)(2,1)}, u32[]{:S(2)}) copy-start(bf16[256,2048]{1,0:T(8,128)(2,1)} %copy-done.12) | copy-start | bytes 3145732
  65.9 32.5 %collective-permute-start.10 = (bf16[2,256,1664]{2,1,0:T(8,128)(2,1)}, bf16[2,256,1664]{2,1,0:T(8,128)(2,1)}, u32[]{:S(2)}, u32[]{:S(2)}) collective-permute-start(bf16[2,256,1664]{2,1,0:T(8,128)(2,1)} %pad_maximum_fusion.1), channel_id=1, source_target_pairs={{0,1},{1,0},{2,3},{3,2},{4,5},{5,4},{6,7},{7,6},{8,9},{9,8},{10,11... | collective-permute-start | bytes 5111816 | tf_op jit(solution)/shard_map/ppermute | solution.py:109
  66.6 4.9 %copy-start.15 = (bf16[1024,2048]{1,0:T(8,128)(2,1)}, bf16[1024,2048]{1,0:T(8,128)(2,1)S(1)}, u32[]{:S(2)}) copy-start(bf16[1024,2048]{1,0:T(8,128)(2,1)S(1)} %constant_dynamic-update-slice_fusion) | copy-start | bytes 12582916
  71.5 1.7 %copy-start.2 = (bf16[1664,1024]{1,0:T(8,128)(2,1)}, bf16[1664,1024]{1,0:T(8,128)(2,1)S(1)}, u32[]{:S(2)}) copy-start(bf16[1664,1024]{1,0:T(8,128)(2,1)S(1)} %multiply_convert_fusion.1) | copy-start | bytes 10223620
  74.2 18.4 %collective-permute-start.8 = (bf16[208,1024]{1,0:T(8,128)(2,1)}, bf16[208,1024]{1,0:T(8,128)(2,1)}, u32[]{:S(2)}, u32[]{:S(2)}) collective-permute-start(bf16[208,1024]{1,0:T(8,128)(2,1)} %get-tuple-element.68), channel_id=1, source_target_pairs={{0,32},{16,48},{32,64},{48,80},{64,96},{80,112},{96,0},{112,16},{1... | collective-permute-start | bytes 1277960 | tf_op jit(solution)/shard_map/ppermute | solution.py:124
  75.8 61.8 %all-to-all-start = ((bf16[4,256,2048]{2,1,0:T(8,128)(2,1)}), bf16[4,256,2048]{2,1,0:T(8,128)(2,1)}, u32[]{:S(2)}, u32[]{:S(2)}) async-start(bf16[4,256,2048]{2,1,0:T(8,128)(2,1)} %copy-done), calls=%async_computation | async-start | bytes 8388608 | tf_op jit(solution)/shard_map/all_to_all | solution.py:104
  80.6 11.8 %copy-start.3 = (bf16[1664,1024]{1,0:T(8,128)(2,1)S(1)}, bf16[1664,1024]{1,0:T(8,128)(2,1)}, u32[]{:S(2)}) copy-start(bf16[1664,1024]{1,0:T(8,128)(2,1)} %copy-done.2) | copy-start | bytes 10223620
  80.6 13.2 %collective-permute-start.9 = (bf16[208,1024]{1,0:T(8,128)(2,1)}, bf16[208,1024]{1,0:T(8,128)(2,1)S(1)}, u32[]{:S(2)}, u32[]{:S(2)}) collective-permute-start(bf16[208,1024]{1,0:T(8,128)(2,1)} %get-tuple-element.67), channel_id=1, source_target_pairs={{0,96},{16,112},{32,0},{48,16},{64,32},{80,48},{96,64},{112,80},{1... | collective-permute-start | bytes 1277960 | tf_op jit(solution)/shard_map/ppermute | solution.py:125
  89.0 15.8 %copy-start.1 = (bf16[1664,1024]{1,0:T(8,128)(2,1)}, bf16[1664,1024]{1,0:T(8,128)(2,1)S(1)}, u32[]{:S(2)}) copy-start(bf16[1664,1024]{1,0:T(8,128)(2,1)S(1)} %multiply_convert_fusion) | copy-start | bytes 10223620
  89.1 9.4 %copy-start.5 = (bf16[256,1664]{1,0:T(8,128)(2,1)S(1)}, bf16[256,1664]{1,0:T(8,128)(2,1)}, u32[]{:S(2)}) copy-start(bf16[256,1664]{1,0:T(8,128)(2,1)} %copy-done.4) | copy-start | bytes 2555908
  89.1 9.4 %copy-start.7 = (bf16[256,1664]{1,0:T(8,128)(2,1)S(1)}, bf16[256,1664]{1,0:T(8,128)(2,1)}, u32[]{:S(2)}) copy-start(bf16[256,1664]{1,0:T(8,128)(2,1)} %copy-done.6) | copy-start | bytes 2555908
  89.1 9.4 %copy-start.9 = (bf16[256,1664]{1,0:T(8,128)(2,1)S(1)}, bf16[256,1664]{1,0:T(8,128)(2,1)}, u32[]{:S(2)}) copy-start(bf16[256,1664]{1,0:T(8,128)(2,1)} %copy-done.8) | copy-start | bytes 2555908
  89.1 9.4 %copy-start.11 = (bf16[256,1664]{1,0:T(8,128)(2,1)S(1)}, bf16[256,1664]{1,0:T(8,128)(2,1)}, u32[]{:S(2)}) copy-start(bf16[256,1664]{1,0:T(8,128)(2,1)} %copy-done.10) | copy-start | bytes 2555908
  89.1 15.7 %collective-permute-start.11 = (bf16[208,1024]{1,0:T(8,128)(2,1)S(1)}, bf16[208,1024]{1,0:T(8,128)(2,1)S(1)}, u32[]{:S(2)}, u32[]{:S(2)}) collective-permute-start(bf16[208,1024]{1,0:T(8,128)(2,1)S(1)} %get-tuple-element.60), channel_id=1, source_target_pairs={{0,32},{16,48},{32,64},{48,80},{64,96},{80,112},{96,0},{112,16},{1... | collective-permute-start | bytes 1277960 | tf_op jit(solution)/shard_map/ppermute | solution.py:124
  89.8 15.0 %collective-permute-start.12 = (bf16[208,1024]{1,0:T(8,128)(2,1)S(1)}, bf16[208,1024]{1,0:T(8,128)(2,1)S(1)}, u32[]{:S(2)}, u32[]{:S(2)}) collective-permute-start(bf16[208,1024]{1,0:T(8,128)(2,1)S(1)} %get-tuple-element.59), channel_id=1, source_target_pairs={{0,96},{16,112},{32,0},{48,16},{64,32},{80,48},{96,64},{112,80},{1... | collective-permute-start | bytes 1277960 | tf_op jit(solution)/shard_map/ppermute | solution.py:125
  95.1 25.1 %collective-permute-start.13 = (bf16[416,1024]{1,0:T(8,128)(2,1)S(1)}, bf16[416,1024]{1,0:T(8,128)(2,1)S(1)}, u32[]{:S(2)}, u32[]{:S(2)}) collective-permute-start(bf16[416,1024]{1,0:T(8,128)(2,1)S(1)} %get-tuple-element.45), channel_id=1, source_target_pairs={{0,32},{16,48},{32,64},{48,80},{64,96},{80,112},{96,0},{112,16},{1... | collective-permute-start | bytes 2555912 | tf_op jit(solution)/shard_map/ppermute | solution.py:133
  96.8 24.4 %collective-permute-start.14 = (bf16[416,1024]{1,0:T(8,128)(2,1)S(1)}, bf16[416,1024]{1,0:T(8,128)(2,1)S(1)}, u32[]{:S(2)}, u32[]{:S(2)}) collective-permute-start(bf16[416,1024]{1,0:T(8,128)(2,1)S(1)} %get-tuple-element.40), channel_id=1, source_target_pairs={{0,96},{16,112},{32,0},{48,16},{64,32},{80,48},{96,64},{112,80},{1... | collective-permute-start | bytes 2555912 | tf_op jit(solution)/shard_map/ppermute | solution.py:133
  100.7 25.7 %collective-permute-start.15 = (bf16[2,128,1664]{2,1,0:T(8,128)(2,1)S(1)}, bf16[2,128,1664]{2,1,0:T(8,128)(2,1)S(1)}, u32[]{:S(2)}, u32[]{:S(2)}) collective-permute-start(bf16[2,128,1664]{2,1,0:T(8,128)(2,1)S(1)} %pad_maximum_fusion.6), channel_id=1, source_target_pairs={{0,2},{1,3},{2,0},{3,1},{4,6},{5,7},{6,4},{7,5},{8,10},{9,11},{10,... | collective-permute-start | bytes 2555912 | tf_op jit(solution)/shard_map/ppermute | solution.py:144
  106.0 36.1 %collective-permute-start.20 = (bf16[416,1024]{1,0:T(8,128)(2,1)}, bf16[416,1024]{1,0:T(8,128)(2,1)S(1)}, u32[]{:S(2)}, u32[]{:S(2)}) collective-permute-start(bf16[416,1024]{1,0:T(8,128)(2,1)} %get-tuple-element.44), channel_id=1, source_target_pairs={{0,96},{16,112},{32,0},{48,16},{64,32},{80,48},{96,64},{112,80},{1... | collective-permute-start | bytes 2555912 | tf_op jit(solution)/shard_map/ppermute | solution.py:133
  121.2 20.9 %collective-permute-start.19 = (bf16[416,1024]{1,0:T(8,128)(2,1)}, bf16[416,1024]{1,0:T(8,128)(2,1)S(1)}, u32[]{:S(2)}, u32[]{:S(2)}) collective-permute-start(bf16[416,1024]{1,0:T(8,128)(2,1)} %get-tuple-element.50), channel_id=1, source_target_pairs={{0,32},{16,48},{32,64},{48,80},{64,96},{80,112},{96,0},{112,16},{1... | collective-permute-start | bytes 2555912 | tf_op jit(solution)/shard_map/ppermute | solution.py:133
  124.0 22.3 %collective-permute-start.18 = (bf16[208,1024]{1,0:T(8,128)(2,1)}, bf16[208,1024]{1,0:T(8,128)(2,1)}, u32[]{:S(2)}, u32[]{:S(2)}) collective-permute-start(bf16[208,1024]{1,0:T(8,128)(2,1)} %select_convert_fusion.1), channel_id=1, source_target_pairs={{0,16},{16,0},{32,48},{48,32},{64,80},{80,64},{96,112},{112,96},{1... | collective-permute-start | bytes 1277960 | tf_op jit(solution)/shard_map/ppermute | solution.py:152
  127.6 19.8 %collective-permute-start.16 = (bf16[128,1664]{1,0:T(8,128)(2,1)}, bf16[128,1664]{1,0:T(8,128)(2,1)}, u32[]{:S(2)}, u32[]{:S(2)}) collective-permute-start(bf16[128,1664]{1,0:T(8,128)(2,1)} %get-tuple-element.53), channel_id=1, source_target_pairs={{0,0},{7,1},{10,2},{13,3},{1,4},{4,5},{11,6},{14,7},{2,8},{5,9},{8... | collective-permute-start | bytes 1277960 | tf_op jit(solution)/shard_map/ppermute | solution.py:159
  135.1 26.2 %collective-permute-start.17 = (bf16[128,1664]{1,0:T(8,128)(2,1)}, bf16[128,1664]{1,0:T(8,128)(2,1)}, u32[]{:S(2)}, u32[]{:S(2)}) collective-permute-start(bf16[128,1664]{1,0:T(8,128)(2,1)} %get-tuple-element.54), channel_id=1, source_target_pairs={{2,0},{5,1},{8,2},{15,3},{3,4},{6,5},{9,6},{12,7},{0,8},{7,9},{10,... | collective-permute-start | bytes 1277960 | tf_op jit(solution)/shard_map/ppermute | solution.py:160
  143.8 19.7 %collective-permute-start.21 = (bf16[208,1024]{1,0:T(8,128)(2,1)S(1)}, bf16[208,1024]{1,0:T(8,128)(2,1)S(1)}, u32[]{:S(2)}, u32[]{:S(2)}) collective-permute-start(bf16[208,1024]{1,0:T(8,128)(2,1)S(1)} %select_convert_fusion), channel_id=1, source_target_pairs={{0,16},{16,0},{32,48},{48,32},{64,80},{80,64},{96,112},{112,96},{1... | collective-permute-start | bytes 1277960 | tf_op jit(solution)/shard_map/ppermute | solution.py:152

commit v4 on v2

--- a/solution.py
+++ b/solution.py
@@ -19,7 +19,6 @@
 TO_PLANE = [(t * 4 + f, f * 4 + (t - f) % 4) for t in range(4) for f in range(4)]
 TO_PLANE_X = [(a, b ^ 2) for a, b in TO_PLANE]
 FROM_PLANE = [(b, a) for a, b in TO_PLANE]
-FROM_PLANE_X = [(b, a) for a, b in TO_PLANE_X]
 CHUNKS = ((0, 1024), (1024, 2048))
 
 
@@ -38,7 +37,7 @@
 COST = pl.CostEstimate(flops=1000, bytes_accessed=1000, transcendentals=0)
 
 
-def tokens_by_width(place, hs, w, block=256):
+def tokens_by_width(place, hs, w, block=512):
     def kernel(place_ref, *refs):
         w_ref, o_ref = refs[-2:]
         o = dot(jnp.concatenate([r[...] for r in refs[:-2]], axis=0), w_ref[...], 1, 0).astype(BF)
@@ -56,9 +55,9 @@
             + [pl.BlockSpec((w.shape[0], block), lambda i, p: (0, i))],
             out_specs=pl.BlockSpec((4, rows, block), lambda i, p: (0, 0, i)),
         ),
-        out_shape=jax.ShapeDtypeStruct((4, rows, n), BF),
+        out_shape=pltpu.HBM((4, rows, n), BF),
         cost_estimate=COST,
-        compiler_params=params(16),
+        compiler_params=params(24),
     )(place, *hs, w)
 
 
@@ -75,6 +74,7 @@
 
     own_a = lax.ppermute(hidden[:half], ("row", "col"), TO_PLANE)
     own_b = lax.ppermute(hidden[half:], ("row", "col"), TO_PLANE_X)
+    (upstream,) = after(own_a, upstream)
     u3 = lax.ppermute(upstream, "row", Z_UP)
     u1 = lax.ppermute(upstream, "row", Z_DOWN)
     g0 = dot(upstream, weight, 1, 1).astype(BF)
@@ -100,10 +100,6 @@
     u2b = lax.ppermute(u1[half:], "row", Z_DOWN)
     g1, g3 = dot(u1, weight, 1, 1).astype(BF), dot(u3, weight, 1, 1).astype(BF)
 
-    o = tokens_by_width(jnp.reshape(z, (1,)).astype(jnp.int32), hs, weight)
-    o_in = lax.all_to_all(o, "row", 0, 0, tiled=True)
-
-    u2a, u2b = after(o, u2a, u2b)
     g2 = dot(jnp.concatenate([u2a, u2b], axis=0), weight, 1, 1).astype(BF)
     g_send = jnp.stack([jnp.where(even, g1, g0), jnp.where(even, g3, g2)])
     g_in = lax.ppermute(g_send, "col", CORE)
@@ -132,15 +128,16 @@
         w1, w3 = lax.optimization_barrier((w1, w3))
         return w1, w3, lax.ppermute(w1, "dp", Y_UP), lax.ppermute(w3, "dp", Y_DOWN)
 
-    was[0], wbs[0] = after(w2a, was[0], wbs[0])
+    o = tokens_by_width(jnp.reshape(z, (1,)).astype(jnp.int32), hs, weight)
+    o, was[0], wbs[0] = lax.optimization_barrier((o, was[0], wbs[0]))
     w1, w3, s1, s3 = second(0)
+    (o,) = after(w3, o)
+    o_in = lax.all_to_all(o, "row", 0, 0, tiled=True)
 
     (g_in,) = after(w3, g_in)
     g0 = jnp.where(even, g0, g1).astype(F32) + g_in[0].astype(F32)
     g1 = jnp.where(even, g2, g3).astype(F32) + g_in[1].astype(F32)
-    keep_a, keep_b = jnp.where(left, g0[:half], g1[:half]), jnp.where(left, g1[half:], g0[half:])
-    send = jnp.stack([jnp.where(left, g1[:half], g0[:half]), jnp.where(left, g0[half:], g1[half:])])
-    send = send.astype(BF)
+    send = jnp.where(left, g1, g0).astype(BF)
     g_x = lax.ppermute(send, "col", XLO)
 
     was[1], wbs[1] = after(send, was[1], wbs[1])
@@ -155,9 +152,8 @@
     x_out, mine0, x0 = over_x(0, s1, s3)
 
     (g_x,) = after(x_out, g_x)
-    g_a, g_b = (keep_a + g_x[0].astype(F32)).astype(BF), (keep_b + g_x[1].astype(F32)).astype(BF)
-    h_a = lax.ppermute(g_a, ("row", "col"), FROM_PLANE)
-    h_b = lax.ppermute(g_b, ("row", "col"), FROM_PLANE_X)
+    g_b = (jnp.where(left, g0, g1) + g_x.astype(F32)).astype(BF)
+    hidden_grad = lax.ppermute(g_b, ("row", "col"), FROM_PLANE)
 
     v1, v3 = after(g_b, v1, v3)
     x_out, mine1, x1 = over_x(1, v1, v3)
@@ -166,7 +162,6 @@
     output = jnp.sum(o_in.astype(F32), axis=0).astype(BF)
 
     weight_grad = jnp.concatenate([mine0 + x0.astype(F32), mine1 + x1.astype(F32)], axis=1)
-    hidden_grad = jnp.concatenate([h_a, h_b], axis=0)
     return (output, hidden_grad, weight_grad)
 
 

time: 177 us -> 174 us (0.983)
  starting transfers between devices: 56.8 us -> 41.9 us
  waiting for transfers between devices: 61.8 us -> 75.5 us
  other arithmetic: 14.8 us -> 18.5 us
  local copies, waits for them, and re-layouts: 8.78 us -> 5.34 us
    ppermute x1, waiting for transfers between devices: 0.01 us -> 15.2 us  [shards(): swapped = lax.ppermute(own, 'col', XLO)]
    ppermute x2, waiting for transfers between devices: 24.5 us -> 13.4 us  [second(): lax.ppermute(w1, 'dp', Y_UP)]
    ppermute x2 -> x1, waiting for transfers between devices: 7.22 us -> 18.1 us  [shards(): hidden_grad = lax.ppermute(g_b, ('row', 'col'), FROM_PLANE)]
    ppermute x1, waiting for transfers between devices: 11.1 us -> 2.04 us  [shards(): u3 = lax.ppermute(upstream, 'row', Z_UP)]
    ppermute x2 -> x1, starting transfers between devices: 11.5 us -> 2.69 us  [shards(): hidden_grad = lax.ppermute(g_b, ('row', 'col'), FROM_PLANE)]
    ppermute x1, waiting for transfers between devices: 0.01 us -> 6.73 us  [shards(): u2a = lax.ppermute(u3[:half], 'row', Z_UP)]
    convert_element_type x1 -> x2, other arithmetic: 0.22 us -> 4.4 us  [the longest x1 2.2 us: shards(): send = jnp.where(left, g1, g0).astype(BF)]
    unnamed x38 -> x17, local copies, waits for them, and re-layouts: 5.37 us -> 1.31 us
  transfers between devices with their start and end apart: 23 -> 22, of which waited for: 8 -> 9; matrix products, arithmetic and copies ran while one was open for 19% -> 22% of each run, Pallas kernels for 6% -> 6%
where the time goes in v4:
time: 174 us; the launch traced here: 173 us
  waiting for transfers between devices  75.5 us (43%)
  starting transfers between devices  41.9 us (24%)
  matrix products  21.1 us (12%)
  other arithmetic  18.5 us (11%)
  Pallas kernels  9.82 us (6%)
  local copies, waits for them, and re-layouts  5.34 us (3%)
    dot_general x6, matrix products, dot(): lax.dot_general(a, b, (((ca,), (cb,)), ((), ())), preferred_element_type=...  21.1 us
    ppermute x1, waiting for transfers between devices, shards(): hidden_grad = lax.ppermute(g_b, ('row', 'col'), FROM_PLANE)  18.1 us
    ppermute x1, waiting for transfers between devices, shards(): swapped = lax.ppermute(own, 'col', XLO)  15.2 us
    ppermute x2, waiting for transfers between devices, second(): lax.ppermute(w1, 'dp', Y_UP)  13.4 us
    pallas_call x1, Pallas kernels, tokens_by_width(): pl.pallas_call(kernel, grid_spec=pltpu.PrefetchScalarGridSpec(num_scalar_...  9.82 us
    ppermute x2, waiting for transfers between devices, over_x(): return (out, jnp.where(low, t[:hf], t[hf:]), lax.ppermute(out, 'dp', XHI))  8.65 us
    ppermute x1, waiting for transfers between devices, shards(): own_a = lax.ppermute(hidden[:half], ('row', 'col'), TO_PLANE)  7.65 us
    ppermute x1, waiting for transfers between devices, shards(): u2a = lax.ppermute(u3[:half], 'row', Z_UP)  6.73 us
  transfers between devices with their start and end apart: 22, of which 9 were waited for; matrix products, arithmetic and copies ran while one was open for 22% of the time, Pallas kernels for 6%

profile of v4, /device:TPU:2, one launch (start us, length us, event | category | flops | bytes accessed | tf_op | source)
XLA Modules:
  0.0 173.3 jit_solution(16358438410939240535)
XLA Ops:
  0.6 1.3 fusion.32
  1.9 5.8 %collective-permute-start = (bf16[128,1664]{1,0:T(8,128)(2,1)S(1)}, bf16[128,1664]{1,0:T(8,128)(2,1)S(1)}, u32[]{:S(2)}, u32[]{:S(2)}) collective-permute-start(bf16[128,1664]{1,0:T(8,128)(2,1)S(1)} %get-tuple-element.88), channel_id=1, source_target_pairs={{0,0},{1,7},{2,10},{3,13},{4,1},{5,4},{6,11},{7,14},{8,2},{9,5},{1... | collective-permute-start | bytes 1277960 | tf_op jit(solution)/shard_map/ppermute | solution.py:75
  7.7 2.5 %collective-permute-start.5 = (bf16[128,1664]{1,0:T(8,128)(2,1)S(1)}, bf16[128,1664]{1,0:T(8,128)(2,1)S(1)}, u32[]{:S(2)}, u32[]{:S(2)}) collective-permute-start(bf16[128,1664]{1,0:T(8,128)(2,1)S(1)} %get-tuple-element.87), channel_id=1, source_target_pairs={{0,2},{1,5},{2,8},{3,15},{4,3},{5,6},{6,9},{7,12},{8,0},{9,7},{10,... | collective-permute-start | bytes 1277960 | tf_op jit(solution)/shard_map/ppermute | solution.py:76
  10.3 7.6 %collective-permute-done = bf16[128,1664]{1,0:T(8,128)(2,1)S(1)} collective-permute-done((bf16[128,1664]{1,0:T(8,128)(2,1)S(1)}, bf16[128,1664]{1,0:T(8,128)(2,1)S(1)}, u32[]{:S(2)}, u32[]{:S(2)}) %collective-permute-start) | collective-permute-done | bytes 426016 | tf_op jit(solution)/shard_map/ppermute | solution.py:75
  17.9 3.2 %collective-permute-start.2 = (bf16[256,2048]{1,0:T(8,128)(2,1)}, bf16[256,2048]{1,0:T(8,128)(2,1)S(1)}, u32[]{:S(2)}, u32[]{:S(2)}) collective-permute-start(bf16[256,2048]{1,0:T(8,128)(2,1)} %param.5), channel_id=1, source_target_pairs={{0,4},{4,8},{8,12},{12,0},{1,5},{5,9},{9,13},{13,1},{2,6},{6,10},{... | collective-permute-start | bytes 3145736 | tf_op jit(solution)/shard_map/ppermute | solution.py:78
  21.1 0.1 collective-permute-start.1
  21.2 0.1 pad_maximum_fusion.3
  21.3 0.4 collective-permute-start.6
  21.8 5.0 %convolution_convert_fusion.2 = bf16[256,1664]{1,0:T(8,128)(2,1)S(1)} fusion(bf16[256,2048]{1,0:T(8,128)(2,1)S(1)} %copy-done.3, bf16[1664,2048]{1,0:T(8,128)(2,1)} %refs_4_.1), kind=kOutput, calls=%fused_computation.18 | convolution fusion | flops 1745256448 | bytes 8716288 | tf_op jit(solution)/shard_map/dot_general | solution.py:26
  26.8 15.2 %collective-permute-done.6 = bf16[2,128,1664]{2,1,0:T(8,128)(2,1)S(1)} collective-permute-done((bf16[2,128,1664]{2,1,0:T(8,128)(2,1)S(1)}, bf16[2,128,1664]{2,1,0:T(8,128)(2,1)S(1)}, u32[]{:S(2)}, u32[]{:S(2)}) %collective-permute-start.6) | collective-permute-done | bytes 852000 | tf_op jit(solution)/shard_map/ppermute | solution.py:82
  42.0 0.2 select_bitcast_fusion.3
  42.2 0.3 pad_maximum_fusion.1
  42.5 0.1 collective-permute-start.7
  42.6 0.2 pad_maximum_fusion.4
  42.8 2.0 %collective-permute-done.2 = bf16[256,2048]{1,0:T(8,128)(2,1)S(1)} collective-permute-done((bf16[256,2048]{1,0:T(8,128)(2,1)}, bf16[256,2048]{1,0:T(8,128)(2,1)S(1)}, u32[]{:S(2)}, u32[]{:S(2)}) %collective-permute-start.2) | collective-permute-done | bytes 1048608 | tf_op jit(solution)/shard_map/ppermute | solution.py:78
  44.9 0.1 collective-permute-start.3
  45.0 3.3 %collective-permute-start.4 = (bf16[128,2048]{1,0:T(8,128)(2,1)S(1)}, bf16[128,2048]{1,0:T(8,128)(2,1)S(1)}, u32[]{:S(2)}, u32[]{:S(2)}) collective-permute-start(bf16[128,2048]{1,0:T(8,128)(2,1)S(1)} %slice.133), channel_id=1, source_target_pairs={{0,12},{4,0},{8,4},{12,8},{1,13},{5,1},{9,5},{13,9},{2,14},{6,2},{... | collective-permute-start | bytes 1572872 | tf_op jit(solution)/shard_map/ppermute | solution.py:100
  48.3 2.1 %convolution_convert_fusion.1 = bf16[256,1664]{1,0:T(8,128)(2,1)S(1)} fusion(bf16[256,2048]{1,0:T(8,128)(2,1)S(1)} %collective-permute-done.2, bf16[1664,2048]{1,0:T(8,128)(2,1)S(1)} %bitcast.106), kind=kOutput, calls=%fused_computation.17 | convolution fusion | flops 1745256448 | bytes 8716288 | tf_op jit(solution)/shard_map/dot_general | solution.py:26
  50.4 2.2 %convolution_convert_fusion.3 = bf16[256,1664]{1,0:T(8,128)(2,1)S(1)} fusion(bf16[256,2048]{1,0:T(8,128)(2,1)S(1)} %collective-permute-done.1, bf16[1664,2048]{1,0:T(8,128)(2,1)S(1)} %bitcast.106), kind=kOutput, calls=%fused_computation.19 | convolution fusion | flops 1745256448 | bytes 8716288 | tf_op jit(solution)/shard_map/dot_general | solution.py:26
  52.7 0.1 select_bitcast_fusion.1
  52.8 6.7 %collective-permute-done.3 = bf16[128,2048]{1,0:T(8,128)(2,1)S(1)} collective-permute-done((bf16[128,2048]{1,0:T(8,128)(2,1)S(1)}, bf16[128,2048]{1,0:T(8,128)(2,1)S(1)}, u32[]{:S(2)}, u32[]{:S(2)}) %collective-permute-start.3) | collective-permute-done | bytes 524320 | tf_op jit(solution)/shard_map/ppermute | solution.py:99
  59.5 2.1 %convolution_convert_fusion = bf16[256,1664]{1,0:T(8,128)(2,1)S(1)} fusion(bf16[1664,2048]{1,0:T(8,128)(2,1)S(1)} %bitcast.106, bf16[128,2048]{1,0:T(8,128)(2,1)S(1)} %collective-permute-done.4, bf16[128,2048]{1,0:T(8,128)(2,1)S(1)} %collective-permute-done.3), kind=kOutput, calls=%fused_computation.16 | convolution fusion | flops 1747353600 | bytes 8716288 | tf_op jit(solution)/shard_map/dot_general | solution.py:26
  61.6 0.1 select_bitcast_fusion
  61.8 1.4 pad_maximum_fusion
  63.2 0.1 constant_dynamic-update-slice_fusion
  63.3 0.5 bitcast_select_fusion
  63.8 4.9 %multiply_convert_fusion.1 = bf16[1664,1024]{1,0:T(8,128)(2,1)S(1)} fusion(bf16[256,1664]{1,0:T(8,128)(2,1)S(1)} %get-tuple-element.45.refs_3_, bf16[256,1664]{1,0:T(8,128)(2,1)S(1)} %get-tuple-element.44.refs_2_, bf16[256,1664]{1,0:T(8,128)(2,1)S(1)} %get-tuple-element.43.refs_1_, bf16[256,1664]{1,0:T(8,128)(2,1)S(1)} %get-tuple-element.42.refs_0_, ...), kind=kOutput, calls=%fused_computation.1 | convolution fusion | flops 3506700288 | bytes 8912896 | tf_op jit(solution)/shard_map/dot_general | solution.py:26
  68.7 0.1 dynamic-slice_bitcast_fusion.8
  68.8 1.6 collective-permute-start.8
  70.4 1.7 collective-permute-start.9
  72.1 4.8 %multiply_convert_fusion = bf16[1664,1024]{1,0:T(8,128)(2,1)S(1)} fusion(bf16[256,1664]{1,0:T(8,128)(2,1)S(1)} %get-tuple-element.45.refs_3_, bf16[256,1664]{1,0:T(8,128)(2,1)S(1)} %get-tuple-element.44.refs_2_, bf16[256,1664]{1,0:T(8,128)(2,1)S(1)} %get-tuple-element.43.refs_1_, bf16[256,1664]{1,0:T(8,128)(2,1)S(1)} %get-tuple-element.42.refs_0_, ...), kind=kOutput, calls=%fused_computation | convolution fusion | flops 3506700288 | bytes 8912896 | tf_op jit(solution)/shard_map/dot_general | solution.py:26
  76.9 1.1 dynamic-slice_bitcast_fusion.5
  78.0 0.3 collective-permute-start.11
  78.3 2.9 %collective-permute-start.12 = (bf16[208,1024]{1,0:T(8,128)(2,1)}, bf16[208,1024]{1,0:T(8,128)(2,1)}, u32[]{:S(2)}, u32[]{:S(2)}) collective-permute-start(bf16[208,1024]{1,0:T(8,128)(2,1)} %get-tuple-element.67), channel_id=1, source_target_pairs={{0,96},{16,112},{32,0},{48,16},{64,32},{80,48},{96,64},{112,80},{1... | collective-permute-start | bytes 1277960 | tf_op jit(solution)/shard_map/ppermute | solution.py:121
  81.2 9.8 %shard_map.58 = bf16[4,256,2048]{2,1,0:T(8,128)(2,1)} custom-call(s32[1]{0:T(128)} %bitcast.21.place_ref, bf16[256,1664]{1,0:T(8,128)(2,1)S(1)} %get-tuple-element.42.refs_0_, bf16[256,1664]{1,0:T(8,128)(2,1)S(1)} %get-tuple-element.43.refs_1_, bf16[256,1664]{1,0:T(8,128)(2,1)S(1)} %get-tuple-element.44.refs_2_, ...), custom_call_target="tpu_custom_call" | custom-call | flops 1000 | bytes 1000 | tf_op jit(solution)/shard_map/pallas_call | solution.py:49
  91.0 1.3 dynamic-slice_bitcast_fusion.2
  92.4 1.2 fusion.26
  93.6 3.2 %collective-permute-start.14 = (bf16[416,1024]{1,0:T(8,128)(2,1)}, bf16[416,1024]{1,0:T(8,128)(2,1)}, u32[]{:S(2)}, u32[]{:S(2)}) collective-permute-start(bf16[416,1024]{1,0:T(8,128)(2,1)} %get-tuple-element.48), channel_id=1, source_target_pairs={{0,96},{16,112},{32,0},{48,16},{64,32},{80,48},{96,64},{112,80},{1... | collective-permute-start | bytes 2555912 | tf_op jit(solution)/shard_map/ppermute | solution.py:129
  96.8 4.9 %all-to-all-start = ((bf16[4,256,2048]{2,1,0:T(8,128)(2,1)}), bf16[4,256,2048]{2,1,0:T(8,128)(2,1)}, u32[]{:S(2)}, u32[]{:S(2)}) async-start(bf16[4,256,2048]{2,1,0:T(8,128)(2,1)} %shard_map.58), calls=%async_computation | async-start | bytes 8388608 | tf_op jit(solution)/shard_map/all_to_all | solution.py:135
  101.7 2.2 %select_convert_fusion = bf16[256,1664]{1,0:T(8,128)(2,1)S(1)} fusion(pred[]{:T(512)S(6)} %eq.20, bf16[2,256,1664]{2,1,0:T(8,128)(2,1)} %collective-permute-done.10, bf16[256,1664]{1,0:T(8,128)(2,1)S(1)} %convolution_convert_fusion.2, bf16[256,1664]{1,0:T(8,128)(2,1)S(1)} %convolution_convert_fusion.3, pred[]{:T(512)S(6)} %eq.19, ...), kind=kLoop, calls=%fused_computation.32 | loop fusion | flops 4259840 | bytes 5963778 | tf_op jit(solution)/shard_map/convert_element_type | solution.py:140
  103.9 0.1 collective-permute-start.15
  104.0 0.2 copy-done.1
  104.2 0.1 dynamic-slice_bitcast_fusion
  104.3 1.5 fusion.28
  105.8 0.1 collective-permute-start.16
  105.9 3.2 %collective-permute-start.17 = (bf16[416,1024]{1,0:T(8,128)(2,1)S(1)}, bf16[416,1024]{1,0:T(8,128)(2,1)S(1)}, u32[]{:S(2)}, u32[]{:S(2)}) collective-permute-start(bf16[416,1024]{1,0:T(8,128)(2,1)S(1)} %get-tuple-element.52), channel_id=1, source_target_pairs={{0,96},{16,112},{32,0},{48,16},{64,32},{80,48},{96,64},{112,80},{1... | collective-permute-start | bytes 2555912 | tf_op jit(solution)/shard_map/ppermute | solution.py:129
  109.1 7.9 %collective-permute-done.13 = bf16[416,1024]{1,0:T(8,128)(2,1)} collective-permute-done((bf16[416,1024]{1,0:T(8,128)(2,1)}, bf16[416,1024]{1,0:T(8,128)(2,1)}, u32[]{:S(2)}, u32[]{:S(2)}) %collective-permute-start.13) | collective-permute-done | bytes 852000 | tf_op jit(solution)/shard_map/ppermute | solution.py:129
  117.0 2.1 %fusion.16 = f32[416,1024]{1,0:T(8,128)S(1)} fusion(bf16[416,1024]{1,0:T(8,128)(2,1)} %collective-permute-done.14, bf16[416,1024]{1,0:T(8,128)(2,1)} %collective-permute-done.13, bf16[4,416,1024]{2,1,0:T(8,128)(2,1)} %bitcast.114, s32[]{:T(128)S(6)} %select_n.160), kind=kLoop, calls=%fused_computation.26 | loop fusion | flops 2129920 | bytes 4259844 | tf_op jit(solution)/shard_map/add | solution.py:147
  119.1 0.1 select_convert_fusion.2
  119.2 3.0 %collective-permute-start.19 = (bf16[208,1024]{1,0:T(8,128)(2,1)S(1)}, bf16[208,1024]{1,0:T(8,128)(2,1)S(1)}, u32[]{:S(2)}, u32[]{:S(2)}) collective-permute-start(bf16[208,1024]{1,0:T(8,128)(2,1)S(1)} %select_convert_fusion.2), channel_id=1, source_target_pairs={{0,16},{16,0},{32,48},{48,32},{64,80},{80,64},{96,112},{112,96},{1... | collective-permute-start | bytes 1277960 | tf_op jit(solution)/shard_map/ppermute | solution.py:149
  122.2 3.7 %collective-permute-done.15 = bf16[256,1664]{1,0:T(8,128)(2,1)S(1)} collective-permute-done((bf16[256,1664]{1,0:T(8,128)(2,1)S(1)}, bf16[256,1664]{1,0:T(8,128)(2,1)S(1)}, u32[]{:S(2)}, u32[]{:S(2)}) %collective-permute-start.15) | collective-permute-done | bytes 852000 | tf_op jit(solution)/shard_map/ppermute | solution.py:141
  125.9 2.2 %add_convert_fusion = bf16[256,1664]{1,0:T(8,128)(2,1)S(1)} fusion(bf16[256,1664]{1,0:T(8,128)(2,1)S(1)} %collective-permute-done.15, pred[]{:T(512)S(6)} %eq.20, bf16[2,256,1664]{2,1,0:T(8,128)(2,1)} %collective-permute-done.10, bf16[256,1664]{1,0:T(8,128)(2,1)S(1)} %convolution_convert_fusion.2, bf16[256,1664]{1,0:T(8,128)(2,1)S(1)} %convolution_convert_fusion.3, ...), kind=kLoop, calls=%fused_computation.31 | loop fusion | flops 5111808 | bytes 6815746 | tf_op jit(solution)/shard_map/convert_element_type | solution.py:155
  128.1 5.5 %collective-permute-done.16 = bf16[416,1024]{1,0:T(8,128)(2,1)S(1)} collective-permute-done((bf16[416,1024]{1,0:T(8,128)(2,1)S(1)}, bf16[416,1024]{1,0:T(8,128)(2,1)S(1)}, u32[]{:S(2)}, u32[]{:S(2)}) %collective-permute-start.16) | collective-permute-done | bytes 852000 | tf_op jit(solution)/shard_map/ppermute | solution.py:129
  133.6 0.4 fusion.17
  134.1 0.1 select_convert_fusion.1
  134.2 2.8 %collective-permute-start.20 = (bf16[208,1024]{1,0:T(8,128)(2,1)S(1)}, bf16[208,1024]{1,0:T(8,128)(2,1)S(1)}, u32[]{:S(2)}, u32[]{:S(2)}) collective-permute-start(bf16[208,1024]{1,0:T(8,128)(2,1)S(1)} %select_convert_fusion.1), channel_id=1, source_target_pairs={{0,16},{16,0},{32,48},{48,32},{64,80},{80,64},{96,112},{112,96},{1... | collective-permute-start | bytes 1277960 | tf_op jit(solution)/shard_map/ppermute | solution.py:149
  137.0 2.7 %collective-permute-start.18 = (bf16[256,1664]{1,0:T(8,128)(2,1)S(1)}, bf16[256,1664]{1,0:T(8,128)(2,1)S(1)}, u32[]{:S(2)}, u32[]{:S(2)}) collective-permute-start(bf16[256,1664]{1,0:T(8,128)(2,1)S(1)} %add_convert_fusion), channel_id=1, source_target_pairs={{0,0},{7,1},{10,2},{13,3},{1,4},{4,5},{11,6},{14,7},{2,8},{5,9},{8... | collective-permute-start | bytes 2555912 | tf_op jit(solution)/shard_map/ppermute | solution.py:156
  139.7 0.2 convert_add_fusion.9
  139.9 8.7 %collective-permute-done.20 = bf16[208,1024]{1,0:T(8,128)(2,1)S(1)} collective-permute-done((bf16[208,1024]{1,0:T(8,128)(2,1)S(1)}, bf16[208,1024]{1,0:T(8,128)(2,1)S(1)}, u32[]{:S(2)}, u32[]{:S(2)}) %collective-permute-start.20) | collective-permute-done | bytes 426016 | tf_op jit(solution)/shard_map/ppermute | solution.py:149
  148.5 0.2 convert_add_fusion.8
  148.7 1.3 pad_maximum_fusion.2
  150.0 18.1 %collective-permute-done.18 = bf16[256,1664]{1,0:T(8,128)(2,1)S(1)} collective-permute-done((bf16[256,1664]{1,0:T(8,128)(2,1)S(1)}, bf16[256,1664]{1,0:T(8,128)(2,1)S(1)}, u32[]{:S(2)}, u32[]{:S(2)}) %collective-permute-start.18) | collective-permute-done | bytes 852000 | tf_op jit(solution)/shard_map/ppermute | solution.py:156
  168.1 4.3 %reduce_sum.12 = bf16[256,2048]{1,0:T(8,128)(2,1)} reduce(bf16[4,256,2048]{2,1,0:T(8,128)(2,1)} %all-to-all-done, bf16[]{:T(256)} %constant.99.clone.1), dimensions={0}, to_apply=%region_0.1 | reduce | flops 1572864 | bytes 5242882 | tf_op jit(solution)/shard_map/reduce_sum | solution.py:162
  172.4 0.9 copy.15
  (33 shorter events, 0.4 us)
Async XLA Ops:
  0.6 21.1 %copy-start.3 = (bf16[256,2048]{1,0:T(8,128)(2,1)S(1)}, bf16[256,2048]{1,0:T(8,128)(2,1)}, u32[]{:S(2)}) copy-start(bf16[256,2048]{1,0:T(8,128)(2,1)} %param.5) | copy-start | bytes 3145732
  1.9 16.0 %collective-permute-start = (bf16[128,1664]{1,0:T(8,128)(2,1)S(1)}, bf16[128,1664]{1,0:T(8,128)(2,1)S(1)}, u32[]{:S(2)}, u32[]{:S(2)}) collective-permute-start(bf16[128,1664]{1,0:T(8,128)(2,1)S(1)} %get-tuple-element.88), channel_id=1, source_target_pairs={{0,0},{1,7},{2,10},{3,13},{4,1},{5,4},{6,11},{7,14},{8,2},{9,5},{1... | collective-permute-start | bytes 1277960 | tf_op jit(solution)/shard_map/ppermute | solution.py:75
  7.7 13.5 %collective-permute-start.5 = (bf16[128,1664]{1,0:T(8,128)(2,1)S(1)}, bf16[128,1664]{1,0:T(8,128)(2,1)S(1)}, u32[]{:S(2)}, u32[]{:S(2)}) collective-permute-start(bf16[128,1664]{1,0:T(8,128)(2,1)S(1)} %get-tuple-element.87), channel_id=1, source_target_pairs={{0,2},{1,5},{2,8},{3,15},{4,3},{5,6},{6,9},{7,12},{8,0},{9,7},{10,... | collective-permute-start | bytes 1277960 | tf_op jit(solution)/shard_map/ppermute | solution.py:76
  17.9 26.9 %collective-permute-start.2 = (bf16[256,2048]{1,0:T(8,128)(2,1)}, bf16[256,2048]{1,0:T(8,128)(2,1)S(1)}, u32[]{:S(2)}, u32[]{:S(2)}) collective-permute-start(bf16[256,2048]{1,0:T(8,128)(2,1)} %param.5), channel_id=1, source_target_pairs={{0,4},{4,8},{8,12},{12,0},{1,5},{5,9},{9,13},{13,1},{2,6},{6,10},{... | collective-permute-start | bytes 3145736 | tf_op jit(solution)/shard_map/ppermute | solution.py:78
  21.1 23.8 %collective-permute-start.1 = (bf16[256,2048]{1,0:T(8,128)(2,1)}, bf16[256,2048]{1,0:T(8,128)(2,1)S(1)}, u32[]{:S(2)}, u32[]{:S(2)}) collective-permute-start(bf16[256,2048]{1,0:T(8,128)(2,1)} %param.5), channel_id=1, source_target_pairs={{0,12},{4,0},{8,4},{12,8},{1,13},{5,1},{9,5},{13,9},{2,14},{6,2},{... | collective-permute-start | bytes 3145736 | tf_op jit(solution)/shard_map/ppermute | solution.py:79
  21.3 20.7 %collective-permute-start.6 = (bf16[2,128,1664]{2,1,0:T(8,128)(2,1)S(1)}, bf16[2,128,1664]{2,1,0:T(8,128)(2,1)S(1)}, u32[]{:S(2)}, u32[]{:S(2)}) collective-permute-start(bf16[2,128,1664]{2,1,0:T(8,128)(2,1)S(1)} %pad_maximum_fusion.3), channel_id=1, source_target_pairs={{0,2},{1,3},{2,0},{3,1},{4,6},{5,7},{6,4},{7,5},{8,10},{9,11},{10,... | collective-permute-start | bytes 2555912 | tf_op jit(solution)/shard_map/ppermute | solution.py:82
  42.0 6.2 %slice-start = ((s8[6815744]{0:T(1024)(128)(4,1)}), s8[4194304]{0:T(1024)(128)(4,1)S(1)}, s32[]{:S(2)}) async-start(s8[6815744]{0:T(1024)(128)(4,1)} %bitcast.105), calls=%async_computation.1 | async-start | bytes 8388608
  42.2 6.1 %slice-start.1 = ((s8[6815744]{0:T(1024)(128)(4,1)}), s8[2621440]{0:T(1024)(128)(4,1)S(1)}, s32[]{:S(2)}) async-start(s8[6815744]{0:T(1024)(128)(4,1)} %bitcast.105), calls=%async_computation.2 | async-start | bytes 5242880
  42.5 20.8 %collective-permute-start.7 = (bf16[2,256,1664]{2,1,0:T(8,128)(2,1)S(1)}, bf16[2,256,1664]{2,1,0:T(8,128)(2,1)S(1)}, u32[]{:S(2)}, u32[]{:S(2)}) collective-permute-start(bf16[2,256,1664]{2,1,0:T(8,128)(2,1)S(1)} %bitcast.115), channel_id=1, source_target_pairs={{0,1},{1,0},{2,3},{3,2},{4,5},{5,4},{6,7},{7,6},{8,9},{9,8},{10,11... | collective-permute-start | bytes 5111816 | tf_op jit(solution)/shard_map/ppermute | solution.py:91
  44.9 14.7 %collective-permute-start.3 = (bf16[128,2048]{1,0:T(8,128)(2,1)S(1)}, bf16[128,2048]{1,0:T(8,128)(2,1)S(1)}, u32[]{:S(2)}, u32[]{:S(2)}) collective-permute-start(bf16[128,2048]{1,0:T(8,128)(2,1)S(1)} %slice.132), channel_id=1, source_target_pairs={{0,4},{4,8},{8,12},{12,0},{1,5},{5,9},{9,13},{13,1},{2,6},{6,10},{... | collective-permute-start | bytes 1572872 | tf_op jit(solution)/shard_map/ppermute | solution.py:99
  45.0 14.5 %collective-permute-start.4 = (bf16[128,2048]{1,0:T(8,128)(2,1)S(1)}, bf16[128,2048]{1,0:T(8,128)(2,1)S(1)}, u32[]{:S(2)}, u32[]{:S(2)}) collective-permute-start(bf16[128,2048]{1,0:T(8,128)(2,1)S(1)} %slice.133), channel_id=1, source_target_pairs={{0,12},{4,0},{8,4},{12,8},{1,13},{5,1},{9,5},{13,9},{2,14},{6,2},{... | collective-permute-start | bytes 1572872 | tf_op jit(solution)/shard_map/ppermute | solution.py:100
  63.1 38.6 %collective-permute-start.10 = (bf16[2,256,1664]{2,1,0:T(8,128)(2,1)}, bf16[2,256,1664]{2,1,0:T(8,128)(2,1)}, u32[]{:S(2)}, u32[]{:S(2)}) collective-permute-start(bf16[2,256,1664]{2,1,0:T(8,128)(2,1)} %pad_maximum_fusion), channel_id=1, source_target_pairs={{0,1},{1,0},{2,3},{3,2},{4,5},{5,4},{6,7},{7,6},{8,9},{9,8},{10,11... | collective-permute-start | bytes 5111816 | tf_op jit(solution)/shard_map/ppermute | solution.py:105
  68.7 23.7 %copy-start.2 = (bf16[1664,1024]{1,0:T(8,128)(2,1)}, bf16[1664,1024]{1,0:T(8,128)(2,1)S(1)}, u32[]{:S(2)}) copy-start(bf16[1664,1024]{1,0:T(8,128)(2,1)S(1)} %multiply_convert_fusion.1) | copy-start | bytes 10223620
  68.8 23.6 %collective-permute-start.8 = (bf16[208,1024]{1,0:T(8,128)(2,1)S(1)}, bf16[208,1024]{1,0:T(8,128)(2,1)S(1)}, u32[]{:S(2)}, u32[]{:S(2)}) collective-permute-start(bf16[208,1024]{1,0:T(8,128)(2,1)S(1)} %get-tuple-element.74), channel_id=1, source_target_pairs={{0,32},{16,48},{32,64},{48,80},{64,96},{80,112},{96,0},{112,16},{1... | collective-permute-start | bytes 1277960 | tf_op jit(solution)/shard_map/ppermute | solution.py:120
  70.4 22.0 %collective-permute-start.9 = (bf16[208,1024]{1,0:T(8,128)(2,1)S(1)}, bf16[208,1024]{1,0:T(8,128)(2,1)S(1)}, u32[]{:S(2)}, u32[]{:S(2)}) collective-permute-start(bf16[208,1024]{1,0:T(8,128)(2,1)S(1)} %get-tuple-element.73), channel_id=1, source_target_pairs={{0,96},{16,112},{32,0},{48,16},{64,32},{80,48},{96,64},{112,80},{1... | collective-permute-start | bytes 1277960 | tf_op jit(solution)/shard_map/ppermute | solution.py:121
  76.9 14.1 %copy-start = (bf16[1664,1024]{1,0:T(8,128)(2,1)}, bf16[1664,1024]{1,0:T(8,128)(2,1)S(1)}, u32[]{:S(2)}) copy-start(bf16[1664,1024]{1,0:T(8,128)(2,1)S(1)} %multiply_convert_fusion) | copy-start | bytes 10223620
  78.0 26.4 %collective-permute-start.11 = (bf16[208,1024]{1,0:T(8,128)(2,1)}, bf16[208,1024]{1,0:T(8,128)(2,1)}, u32[]{:S(2)}, u32[]{:S(2)}) collective-permute-start(bf16[208,1024]{1,0:T(8,128)(2,1)} %get-tuple-element.68), channel_id=1, source_target_pairs={{0,32},{16,48},{32,64},{48,80},{64,96},{80,112},{96,0},{112,16},{1... | collective-permute-start | bytes 1277960 | tf_op jit(solution)/shard_map/ppermute | solution.py:120
  78.3 26.0 %collective-permute-start.12 = (bf16[208,1024]{1,0:T(8,128)(2,1)}, bf16[208,1024]{1,0:T(8,128)(2,1)}, u32[]{:S(2)}, u32[]{:S(2)}) collective-permute-start(bf16[208,1024]{1,0:T(8,128)(2,1)} %get-tuple-element.67), channel_id=1, source_target_pairs={{0,96},{16,112},{32,0},{48,16},{64,32},{80,48},{96,64},{112,80},{1... | collective-permute-start | bytes 1277960 | tf_op jit(solution)/shard_map/ppermute | solution.py:121
  93.6 23.4 %collective-permute-start.13 = (bf16[416,1024]{1,0:T(8,128)(2,1)}, bf16[416,1024]{1,0:T(8,128)(2,1)}, u32[]{:S(2)}, u32[]{:S(2)}) collective-permute-start(bf16[416,1024]{1,0:T(8,128)(2,1)} %get-tuple-element.53), channel_id=1, source_target_pairs={{0,32},{16,48},{32,64},{48,80},{64,96},{80,112},{96,0},{112,16},{1... | collective-permute-start | bytes 2555912 | tf_op jit(solution)/shard_map/ppermute | solution.py:129
  93.6 23.4 %collective-permute-start.14 = (bf16[416,1024]{1,0:T(8,128)(2,1)}, bf16[416,1024]{1,0:T(8,128)(2,1)}, u32[]{:S(2)}, u32[]{:S(2)}) collective-permute-start(bf16[416,1024]{1,0:T(8,128)(2,1)} %get-tuple-element.48), channel_id=1, source_target_pairs={{0,96},{16,112},{32,0},{48,16},{64,32},{80,48},{96,64},{112,80},{1... | collective-permute-start | bytes 2555912 | tf_op jit(solution)/shard_map/ppermute | solution.py:129
  96.8 71.3 %all-to-all-start = ((bf16[4,256,2048]{2,1,0:T(8,128)(2,1)}), bf16[4,256,2048]{2,1,0:T(8,128)(2,1)}, u32[]{:S(2)}, u32[]{:S(2)}) async-start(bf16[4,256,2048]{2,1,0:T(8,128)(2,1)} %shard_map.58), calls=%async_computation | async-start | bytes 8388608 | tf_op jit(solution)/shard_map/all_to_all | solution.py:135
  101.7 2.5 %copy-start.1 = (bf16[1664,1024]{1,0:T(8,128)(2,1)S(1)}, bf16[1664,1024]{1,0:T(8,128)(2,1)}, u32[]{:S(2)}) copy-start(bf16[1664,1024]{1,0:T(8,128)(2,1)} %copy-done) | copy-start | bytes 10223620
  103.9 22.0 %collective-permute-start.15 = (bf16[256,1664]{1,0:T(8,128)(2,1)S(1)}, bf16[256,1664]{1,0:T(8,128)(2,1)S(1)}, u32[]{:S(2)}, u32[]{:S(2)}) collective-permute-start(bf16[256,1664]{1,0:T(8,128)(2,1)S(1)} %select_convert_fusion), channel_id=1, source_target_pairs={{0,2},{1,3},{2,0},{3,1},{4,6},{5,7},{6,4},{7,5},{8,10},{9,11},{10,... | collective-permute-start | bytes 2555912 | tf_op jit(solution)/shard_map/ppermute | solution.py:141
  105.8 27.8 %collective-permute-start.16 = (bf16[416,1024]{1,0:T(8,128)(2,1)S(1)}, bf16[416,1024]{1,0:T(8,128)(2,1)S(1)}, u32[]{:S(2)}, u32[]{:S(2)}) collective-permute-start(bf16[416,1024]{1,0:T(8,128)(2,1)S(1)} %get-tuple-element.57), channel_id=1, source_target_pairs={{0,32},{16,48},{32,64},{48,80},{64,96},{80,112},{96,0},{112,16},{1... | collective-permute-start | bytes 2555912 | tf_op jit(solution)/shard_map/ppermute | solution.py:129
  105.9 27.7 %collective-permute-start.17 = (bf16[416,1024]{1,0:T(8,128)(2,1)S(1)}, bf16[416,1024]{1,0:T(8,128)(2,1)S(1)}, u32[]{:S(2)}, u32[]{:S(2)}) collective-permute-start(bf16[416,1024]{1,0:T(8,128)(2,1)S(1)} %get-tuple-element.52), channel_id=1, source_target_pairs={{0,96},{16,112},{32,0},{48,16},{64,32},{80,48},{96,64},{112,80},{1... | collective-permute-start | bytes 2555912 | tf_op jit(solution)/shard_map/ppermute | solution.py:129
  119.2 20.5 %collective-permute-start.19 = (bf16[208,1024]{1,0:T(8,128)(2,1)S(1)}, bf16[208,1024]{1,0:T(8,128)(2,1)S(1)}, u32[]{:S(2)}, u32[]{:S(2)}) collective-permute-start(bf16[208,1024]{1,0:T(8,128)(2,1)S(1)} %select_convert_fusion.2), channel_id=1, source_target_pairs={{0,16},{16,0},{32,48},{48,32},{64,80},{80,64},{96,112},{112,96},{1... | collective-permute-start | bytes 1277960 | tf_op jit(solution)/shard_map/ppermute | solution.py:149
  134.2 14.3 %collective-permute-start.20 = (bf16[208,1024]{1,0:T(8,128)(2,1)S(1)}, bf16[208,1024]{1,0:T(8,128)(2,1)S(1)}, u32[]{:S(2)}, u32[]{:S(2)}) collective-permute-start(bf16[208,1024]{1,0:T(8,128)(2,1)S(1)} %select_convert_fusion.1), channel_id=1, source_target_pairs={{0,16},{16,0},{32,48},{48,32},{64,80},{80,64},{96,112},{112,96},{1... | collective-permute-start | bytes 1277960 | tf_op jit(solution)/shard_map/ppermute | solution.py:149
  137.0 31.2 %collective-permute-start.18 = (bf16[256,1664]{1,0:T(8,128)(2,1)S(1)}, bf16[256,1664]{1,0:T(8,128)(2,1)S(1)}, u32[]{:S(2)}, u32[]{:S(2)}) collective-permute-start(bf16[256,1664]{1,0:T(8,128)(2,1)S(1)} %add_convert_fusion), channel_id=1, source_target_pairs={{0,0},{7,1},{10,2},{13,3},{1,4},{4,5},{11,6},{14,7},{2,8},{5,9},{8... | collective-permute-start | bytes 2555912 | tf_op jit(solution)/shard_map/ppermute | solution.py:156
